TPU v7x, 256 devices: a whole 4x4x8 slice. The times are simulated.
256 devices in a mesh: dp: 2 (over core), mx: 16 (over y, x), my: 8 (over z).
Axes of the slice: x: 4, y: 4, z: 8, core: 2. Of those that a mesh axis runs over, the one named last changes fastest.
Arguments:
- patches: bfloat16 [1024, 6144], P('dp', 'mx'), may hold values from -40 to 40
- ln_gain: float32 [6144], P('mx'), may hold values from 0.5 to 2
- w_qkv: bfloat16 [3, 6144, 6144], P(None, 'mx', 'my'), may hold values from -1 to 1, as said below
- qk_gain: float32 [2, 6144], P(None, 'my'), may hold values from 0 to 6
- w_out: bfloat16 [6144, 6144], P('my', 'mx'), may hold values from -0.078125 to 0.078125
- w_up: bfloat16 [6144, 24576], P('mx', 'my'), may hold values from -0.078125 to 0.078125
- w_down: bfloat16 [24576, 6144], P('my', 'mx'), may hold values from -0.0390625 to 0.0390625
- w_adapt: bfloat16 [6144, 4096], P('mx', 'my'), may hold values from -0.078125 to 0.078125
- patch_counts: int32 [2, 2], P('dp'), may hold values from 1 to 256, 384 in all within a row
Outputs:
- encoded: bfloat16 [768, 4096], P(('dp', 'mx', 'my'))
Inputs may be any that keep to these rules, and one draw needn't show every extreme that they name: `w_qkv`: entries scaled by the inverse square root of 6144.
All inputs are finite; a program needn't handle non-finite values.
Results may differ from a plain program's by a relative error of at most 0.027.
Values may be sent and summed in bfloat16 or wider, within the bound.
A program may use at most 64 MiB of HBM per device.

v0:
```python
import jax
import jax.numpy as jnp
from jax import lax
from jax.sharding import PartitionSpec as P

D = 6144
HD = 128
PATCHES = 256
IMG_DP = 2
SLOTS_DP = 384


def row_norm(values, gain):
    mean = jnp.mean(values, -1, keepdims=True)
    square = jnp.mean(values * values, -1, keepdims=True)
    return (values - mean) * lax.rsqrt(square - mean * mean + 1e-06) * gain


def finish(projected, lifted, qk_gain):
    count = projected.shape[0]
    width = projected.shape[2]
    heads = width // HD
    gains = qk_gain.reshape(2, heads, HD)
    queries = row_norm(projected[:, 0].reshape(count, heads, HD), gains[0]).reshape(count, width)
    keys = row_norm(projected[:, 1].reshape(count, heads, HD), gains[1]).reshape(count, width)
    joined = jnp.stack([queries, keys, projected[:, 2]], axis=1).astype(jnp.bfloat16)
    hidden = jax.nn.gelu(lifted, approximate=False).astype(jnp.bfloat16)
    return (joined, hidden)


def attend(joined):
    total = joined.shape[0]
    width = joined.shape[2]
    heads = width // HD
    parts = joined.reshape(IMG_DP, total // IMG_DP, 3, heads, HD)
    scores = jnp.einsum(
        "iphd,iqhd->ihpq", parts[:, :, 0], parts[:, :, 1], preferred_element_type=jnp.float32
    )
    scores = scores * HD ** (-0.5)
    top = jnp.max(scores, -1, keepdims=True)
    expo = jnp.exp(scores - top)
    weights = (expo / jnp.sum(expo, -1, keepdims=True)).astype(jnp.bfloat16)
    attended = jnp.einsum(
        "ihpq,iqhd->iphd", weights, parts[:, :, 2], preferred_element_type=jnp.float32
    )
    return attended.astype(jnp.bfloat16).reshape(total, width)


def slot_sources(counts):
    ends = jnp.cumsum(counts)
    starts = ends - counts
    slot = jnp.arange(SLOTS_DP)
    image = jnp.sum((ends[None, :] <= slot[:, None]).astype(jnp.int32), axis=1)
    which = image[:, None] == jnp.arange(IMG_DP)[None, :]
    start = jnp.sum(jnp.where(which, starts[None, :], 0), axis=1)
    return image * PATCHES + slot - start


def per_device(patches, ln_gain, w_qkv, qk_gain, w_out, w_up, w_down, w_adapt, patch_counts):
    tokens_f = patches.astype(jnp.float32)
    first, second = lax.psum((jnp.sum(tokens_f, 1), jnp.sum(tokens_f * tokens_f, 1)), "mx")
    mean = (first / D)[:, None]
    square = (second / D)[:, None]
    normed = ((tokens_f - mean) * lax.rsqrt(square - mean * mean + 1e-06) * ln_gain).astype(
        jnp.bfloat16
    )
    projected_part = jnp.einsum("rd,kdc->rkc", normed, w_qkv, preferred_element_type=jnp.float32)
    lifted_part = jnp.dot(normed, w_up, preferred_element_type=jnp.float32)
    projected, lifted = (
        lax.psum(projected_part.astype(jnp.bfloat16), "mx").astype(jnp.float32),
        lax.psum(lifted_part.astype(jnp.bfloat16), "mx").astype(jnp.float32),
    )
    joined, hidden = finish(projected, lifted, qk_gain)
    attended = attend(joined)
    branches = jnp.dot(attended, w_out, preferred_element_type=jnp.float32)
    branches = branches + jnp.dot(hidden, w_down, preferred_element_type=jnp.float32)
    branches = lax.psum(branches.astype(jnp.bfloat16), "my").astype(jnp.float32)
    updated = (tokens_f + branches).astype(jnp.bfloat16)
    sources = slot_sources(patch_counts[0])
    blocks = lax.axis_size("my")
    owned = sources.shape[0] // (lax.axis_size("mx") * blocks)
    adapted = lax.psum(
        jnp.dot(updated, w_adapt, preferred_element_type=jnp.float32).astype(jnp.bfloat16), "mx"
    ).astype(jnp.float32)
    mine = lax.dynamic_slice_in_dim(
        sources, lax.axis_index("mx") * (blocks * owned), blocks * owned
    )
    routed = adapted[mine].astype(jnp.bfloat16).reshape(blocks, owned, adapted.shape[1])
    moved = lax.all_to_all(routed, "my", split_axis=0, concat_axis=2, tiled=True)
    return moved.reshape(owned, moved.shape[2])


def solution(mesh):
    return jax.shard_map(
        per_device,
        mesh=mesh,
        in_specs=(
            P("dp", "mx"),
            P("mx"),
            P(None, "mx", "my"),
            P(None, "my"),
            P("my", "mx"),
            P("mx", "my"),
            P("my", "mx"),
            P("mx", "my"),
            P("dp", None),
        ),
        out_specs=P(("dp", "mx", "my"), None),
        check_vma=False,
    )
```

profile of v0, /device:TPU:2, one launch (start us, length us, event | category | flops | bytes accessed | tf_op | source)
XLA Modules:
  0.0 443.0 jit_solution(11820477192865632253)
XLA Ops:
  6.5 0.0 copy-start
  6.5 0.0 copy-start.2
  6.5 0.0 copy-start.10
  6.5 0.0 all-reduce.10.cloned.1.call-start
  6.5 1.4 convert_reduce_fusion
  7.9 37.7 %all-reduce = (f32[512]{0:T(512)S(1)}, f32[512]{0:T(512)S(1)}) all-reduce(f32[512]{0:T(512)S(1)} %get-tuple-element.10, f32[512]{0:T(512)S(1)} %get-tuple-element.9), channel_id=1, replica_groups=mesh['dp'=2,'mx'=16,'my'=8] {'mx'}, use_global_device_ids=true, to_apply=%region_3.0 | all-reduce | flops 1024 | bytes 8192 | tf_op jit(solution)/shard_map/psum | solution.py:61
  45.7 4.5 %convolution_convert_fusion.1 = bf16[512,3,768]{2,0,1:T(8,128)(2,1)} fusion(bf16[3,384,768]{2,1,0:T(8,128)(2,1)} %param.11, bf16[512,384]{1,0:T(8,128)(2,1)} %param.9, f32[384]{0:T(512)} %param.10, f32[512]{0:T(512)S(1)} %get-tuple-element.26, f32[512]{0:T(512)S(1)} %get-tuple-element.25), kind=kOutput, calls=%fused_computation.42 | convolution fusion | flops 908132352 | bytes 4527616 | tf_op jit(solution)/shard_map/rd,kdc->rkc/dot_general | solution.py:67
  50.1 0.0 copy-done
  50.1 0.0 copy-done.2
  50.1 0.0 copy-done.10
  50.1 0.0 copy-start.7
  50.1 3.5 convolution_convert_fusion
  53.7 0.0 all-reduce.10.cloned.1.call-update
  53.7 0.0 all-reduce.6.cloned.1.call-start
  53.7 0.0 copy-done.7
  53.8 126.3 %all-reduce.10.cloned.1.call-done = (bf16[512,3072]{1,0:T(8,128)(2,1)}, bf16[512,3,768]{2,0,1:T(8,128)(2,1)}) async-done(((bf16[512,3072]{1,0:T(8,128)(2,1)}, bf16[512,3,768]{2,0,1:T(8,128)(2,1)}), (bf16[512,3072]{1,0:T(8,128)(2,1)}, bf16[512,3,768]{2,0,1:T(8,128)(2,1)})) %all-reduce.10.cloned.1.call-update) | async-done | bytes 5505040 | tf_op jit(solution)/shard_map/psum | solution.py:71
  180.1 1.3 slice.28
  181.5 3.3 fusion.91
  184.7 0.0 copy-done.1
  184.7 2.5 convert_element_type.60
  187.2 1.9 reshape.111
  189.1 3.1 copy.30
  192.2 3.1 copy.34
  195.3 2.4 fusion.89
  197.7 1.4 sub.72
  199.1 3.1 copy.35
  202.2 1.3 sub.68
  203.5 3.0 copy.31
  206.6 1.4 mul.143
  208.0 3.0 copy.36
  211.0 1.3 mul.135
  212.3 3.1 copy.32
  215.4 5.5 %multiply_convert_fusion.1 = (bf16[512,1,768]{2,0,1:T(8,128)(2,1)}, bf16[512,1,768]{2,0,1:T(8,128)(2,1)}) fusion(f32[512,1,768]{2,0,1:T(8,128)} %copy.32, f32[512,1,768]{2,0,1:T(8,128)} %copy.31, f32[768]{0:T(1024)S(1)} %get-tuple-element.11, f32[512,3,768]{2,0,1:T(8,128)} %convert_element_type.60, f32[768]{0:T(1024)S(1)} %get-tuple-element.12, ...), kind=kLoop, calls=%fused_computation.46 | loop fusion | flops 3145728 | bytes 11016192 | tf_op jit(solution)/shard_map/convert.6
  220.9 2.0 reshape.112
  222.9 2.7 reshape.113
  225.7 1.9 fusion.47
  227.5 2.5 fusion.92
  230.0 0.0 copy-done.4
  230.0 0.0 copy-start.8
  230.1 0.0 copy-start.9
  230.1 0.5 fusion.40
  230.6 0.8 copy.42
  231.4 0.2 copy.50
  231.6 0.4 copy-done.8
  231.9 0.7 copy-done.9
  232.7 15.3 %fusion.32 = f32[512,384]{1,0:T(8,128)S(1)} fusion(bf16[3072,384]{1,0:T(8,128)(2,1)S(1)} %copy-done.9, bf16[512,3072]{1,0:T(8,128)(2,1)S(1)} %copy-done.8), kind=kOutput, calls=%fused_computation.39 | convolution fusion | flops 1311768576 | bytes 6291456 | tf_op jit(solution)/shard_map/dot_general | solution.py:76
  248.0 0.0 copy-done.5
  248.0 1.4 fusion.41
  249.3 0.0 all-reduce.6.cloned.1.call-update
  249.4 0.0 all-reduce.8.cloned.1.call-start
  249.4 0.0 copy-done.11
  249.4 0.2 reduce-window.4
  249.6 0.1 fusion.53
  249.7 72.7 %all-reduce.6.cloned.1.call-done = bf16[512,384]{1,0:T(8,128)(2,1)} async-done(((bf16[512,384]{1,0:T(8,128)(2,1)}), bf16[512,384]{1,0:T(8,128)(2,1)}) %all-reduce.6.cloned.1.call-update) | async-done | bytes 393232 | tf_op jit(solution)/shard_map/psum | solution.py:77
  322.4 0.0 copy-done.3
  322.4 0.0 copy-done.6
  322.4 2.2 convolution_convert_fusion.2
  324.6 0.0 all-reduce.8.cloned.1.call-update
  324.6 0.1 fusion.54
  324.7 0.1 compare_select_fusion.1
  324.8 94.4 %all-reduce.8.cloned.1.call-done = bf16[512,512]{1,0:T(8,128)(2,1)} async-done(((bf16[512,512]{1,0:T(8,128)(2,1)}), bf16[512,512]{1,0:T(8,128)(2,1)}) %all-reduce.8.cloned.1.call-update) | async-done | bytes 524304 | tf_op jit(solution)/shard_map/psum | solution.py:82
  419.3 1.7 gather_fusion
  421.0 14.8 %all_to_all.15 = bf16[8,3,512]{2,1,0:T(4,128)(2,1)S(1)} all-to-all(bf16[8,3,512]{2,1,0:T(4,128)(2,1)S(1)} %convert_element_type.74), channel_id=1, replica_groups=mesh['dp'=2,'mx'=16,'my'=8] {'my'}, dimensions={0} | all-to-all | bytes 49152 | tf_op jit(solution)/shard_map/all_to_all | solution.py:89
  435.8 0.6 copy.62
  (14 shorter events, 0.1 us)
Async XLA Ops:
  6.5 43.6 %copy-start = (bf16[384,3072]{1,0:T(8,128)(2,1)S(1)}, bf16[384,3072]{1,0:T(8,128)(2,1)}, u32[]{:S(2)}) copy-start(bf16[384,3072]{1,0:T(8,128)(2,1)} %param.14) | copy-start | bytes 7077892
  6.5 43.6 %copy-start.2 = (bf16[512,384]{1,0:T(8,128)(2,1)S(1)}, bf16[512,384]{1,0:T(8,128)(2,1)}, u32[]{:S(2)}) copy-start(bf16[512,384]{1,0:T(8,128)(2,1)} %param.9) | copy-start | bytes 1179652
  6.5 43.6 %copy-start.10 = (f32[384]{0:T(512)S(1)}, f32[384]{0:T(512)}, u32[]{:S(2)}) copy-start(f32[384]{0:T(512)} %param.10) | copy-start | bytes 4612
  6.5 173.6 %all-reduce.10.cloned.1.call-start = ((), (), s32[]{:S(2)}) async-start(), calls=%async_computation.3 | async-start | bytes 11010048 | tf_op jit(solution)/shard_map/psum | solution.py:71
  50.1 3.6 copy-start.7
  53.7 268.7 %all-reduce.6.cloned.1.call-start = ((), (), s32[]{:S(2)}) async-start(), calls=%async_computation.1 | async-start | bytes 786432 | tf_op jit(solution)/shard_map/psum | solution.py:77
  180.1 4.6 %copy-start.1 = (bf16[512,3,768]{2,0,1:T(8,128)(2,1)S(1)}, bf16[512,3,768]{2,0,1:T(8,128)(2,1)}, u32[]{:S(2)}) copy-start(bf16[512,3,768]{2,0,1:T(8,128)(2,1)} %get-tuple-element.16) | copy-start | bytes 7077892
  225.7 4.4 copy-start.4
  230.0 1.9 copy-start.8
  230.1 2.6 copy-start.9
  232.7 15.3 %copy-start.5 = (bf16[768,384]{1,0:T(8,128)(2,1)S(1)}, bf16[768,384]{1,0:T(8,128)(2,1)}, u32[]{:S(2)}) copy-start(bf16[768,384]{1,0:T(8,128)(2,1)} %param.13) | copy-start | bytes 1769476
  232.7 16.8 %copy-start.11 = (s32[1,2]{1,0:T(1,128)S(1)}, s32[1,2]{1,0:T(1,128)}, u32[]{:S(2)}) copy-start(s32[1,2]{1,0:T(1,128)} %param.17) | copy-start | bytes 28
  232.7 89.7 %copy-start.3 = (bf16[512,384]{1,0:T(8,128)(2,1)S(1)}, bf16[512,384]{1,0:T(8,128)(2,1)}, u32[]{:S(2)}) copy-start(bf16[512,384]{1,0:T(8,128)(2,1)} %param.9) | copy-start | bytes 1179652
  232.7 89.7 %copy-start.6 = (bf16[384,512]{1,0:T(8,128)(2,1)S(1)}, bf16[384,512]{1,0:T(8,128)(2,1)}, u32[]{:S(2)}) copy-start(bf16[384,512]{1,0:T(8,128)(2,1)} %param.16) | copy-start | bytes 1179652
  249.4 169.9 %all-reduce.8.cloned.1.call-start = ((), (), s32[]{:S(2)}) async-start(), calls=%async_computation.2 | async-start | bytes 1048576 | tf_op jit(solution)/shard_map/psum | solution.py:82
Sparse Core Ops, SparseCore 0:
  53.8 126.2 all-reduce.9
  249.5 72.8 all-reduce.5
  325.9 93.2 all-reduce.7
where the time goes:
time: 443 us
  waiting for transfers between devices  294 us (66%)
  blocking collectives  52.6 us (12%)
  local copies, waits for them, and re-layouts  39.6 us (9%)
  matrix products  29.3 us (7%)
  other arithmetic  14.7 us (3%)
  between operations  13.3 us (3%)
    psum x1, waiting for transfers between devices, per_device(): lax.psum(lifted_part.astype(jnp.bfloat16), 'mx').astype(jnp.float32)  126 us
    psum x1, waiting for transfers between devices, per_device(): lax.psum(jnp.dot(updated, w_adapt, preferred_element_type=jnp.float32).as...  94.4 us
    psum x1, waiting for transfers between devices, per_device(): branches = lax.psum(branches.astype(jnp.bfloat16), 'my').astype(jnp.float32)  72.7 us
    psum x1, blocking collectives, per_device(): lax.psum((jnp.sum(tokens_f, 1), jnp.sum(tokens_f * tokens_f, 1)), 'mx')  37.7 us
    dot_general x1, matrix products, per_device(): jnp.dot(hidden, w_down, preferred_element_type=jnp.float32)  15.3 us
    all_to_all x1, blocking collectives, per_device(): lax.all_to_all(routed, 'my', split_axis=0, concat_axis=2, tiled=True)  14.8 us
  transfers between devices with their start and end apart: 3, of which 3 were waited for; matrix products, arithmetic and copies ran while one was open for 0% of the time, Pallas kernels for 0%

commit v1 on v0

v1 whole, which is shorter than its diff:
```python
import jax
import jax.numpy as jnp
from jax import lax
from jax.experimental import pallas as pl
from jax.experimental.pallas import tpu as pltpu
from jax.sharding import PartitionSpec as P

MESH = pl.DeviceIdType.MESH
D = 6144
HD = 128
F32 = jnp.float32
BF16 = jnp.bfloat16

K0, V0, Q0, M0, UNITS = 0, 4, 8, 11, 23


def dot(a, b):
    return jnp.dot(a, b, preferred_element_type=F32)


def dot_t(a, b):
    return lax.dot_general(a, b, (((1,), (1,)), ((), ())), preferred_element_type=F32)


def kernel(
    x_hbm, gain_ref, wqkv_hbm, qkg_ref, wout_hbm, wup_hbm, wdown_hbm, wad_hbm, cnt_ref,
    out_ref,
    x, a, wv, wd, wa, stat, acc, snd, rcv, kv, qn, agb, zs, bsum, zr, xz, tr, fs, fr,
    sem_x, sem_wv, sem_wd, sem_wa,
    stat_s, stat_r, rs_s, rs_r, kv_s, kv_r, ag_s, ag_r, z_s, z_r, f_s, f_r, wz_s, wz_r, wc_s, wc_r,
):
    dp, mx, z = lax.axis_index("dp"), lax.axis_index("mx"), lax.axis_index("my")
    cy, cx = mx // 4, mx % 4
    vx, vy = cx // 2, cy // 2
    ux = cx % 2 + vx - 2 * (cx % 2) * vx
    uy = cy % 2 + vy - 2 * (cy % 2) * vy
    bits = (ux, uy, vx, vy)
    drow = ux * 4 + uy * 2 + vx
    halves = (vy, 1 - vy)

    def flip(c):
        return c + 1 - 2 * (c % 2)

    partners = (
        (dp, cy * 4 + flip(cx), z),
        (dp, flip(cy) * 4 + cx, z),
        (dp, cy * 4 + 3 - cx, z),
        (dp, (3 - cy) * 4 + cx, z),
    )
    plane = [((cy + o // 4) % 4) * 4 + (cx + o % 4) % 4 for o in range(1, 16)]
    column = [(z + o) % 8 for o in range(1, 8)]
    other = (1 - dp, mx, z)

    def relative(block):
        total = 0
        for bit, weight in ((block // 4, 4), ((block // 2) % 2, 2), (block % 2, 1)):
            own = bits[{4: 0, 2: 1, 1: 2}[weight]]
            total = total + weight * (bit + own - 2 * bit * own)
        return total

    sent = []

    def remote(src, dst, s, r, device):
        return pltpu.make_async_remote_copy(
            src_ref=src, dst_ref=dst, send_sem=s, recv_sem=r, device_id=device, device_id_type=MESH
        )

    def start(copy):
        copy.start()
        sent.append(copy)

    load_x = pltpu.make_async_copy(x_hbm, x, sem_x)
    load_x.start()
    load_wv, load_wd = {}, {}

    def half_at(base, half):
        return pl.ds(pl.multiple_of(base + half * 384, 128), 384)

    for i in (1, 2, 0, 3, 4, 5, 6):
        for h in range(2):
            if i < 3:
                src = wqkv_hbm.at[i, :, half_at(0, halves[h])]
            else:
                src = wup_hbm.at[:, half_at((i - 3) * 768, halves[h])]
            load_wv[i, h] = pltpu.make_async_copy(src, wv.at[i, h], sem_wv.at[i, h])
            load_wv[i, h].start()
    load_wa = pltpu.make_async_copy(wad_hbm, wa.at[z], sem_wa)
    load_wa.start()
    for i in range(5):
        for h in range(2):
            src = wdown_hbm.at[half_at(i * 768, halves[h])] if i < 4 else wout_hbm.at[half_at(0, halves[h])]
            load_wd[i, h] = pltpu.make_async_copy(src, wd.at[i, h], sem_wd.at[i, h])
            load_wd[i, h].start()

    barrier = pltpu.get_barrier_semaphore()
    greet = [(dp, m, z) for m in plane] + [(dp, mx, c) for c in column] + [other]
    for device in greet:
        pl.semaphore_signal(barrier, inc=1, device_id=device, device_id_type=MESH)

    load_x.wait()
    xb = x[...]
    xf = xb.astype(F32)
    x2 = xf * xf
    hi = x2.astype(BF16)
    lo = (x2 - hi.astype(F32)).astype(BF16)
    row8 = lax.broadcasted_iota(jnp.int32, (8, 384), 0)
    e0 = (row8 == 0).astype(F32).astype(BF16)
    e1 = (row8 == 1).astype(F32).astype(BF16)
    stat[0] = (dot_t(e0, xb) + dot_t(e1, hi) + dot_t(e1, lo))[0:2]

    pl.semaphore_wait(barrier, len(greet))
    for o in range(15):
        start(remote(stat.at[0], stat.at[o + 1], stat_s.at[o], stat_r, (dp, plane[o], z)))
    mine = pl.ds(pl.multiple_of(dp * 192, 16), 192)
    for o in range(7):
        start(remote(wad_hbm.at[mine], wa.at[z, mine], wz_s.at[o], wz_r, (dp, mx, column[o])))

    c0 = cnt_ref[0, 0]

    def pick(slot, width):
        token = slot + jnp.where(slot >= c0, 256 - c0, 0)
        lane = lax.broadcasted_iota(jnp.int32, token.shape, 1)
        parts = [
            jnp.where(token == lane + 128 * j, 1.0, 0.0).astype(BF16) for j in range(width // 128)
        ]
        return jnp.concatenate(parts, axis=1)

    row = lax.broadcasted_iota(jnp.int32, (384, 128), 0)
    block = jnp.bitwise_xor((row >> 4) & 7, drow)
    chosen = pick((row & 15) * 24 + block * 3 + (row >> 7), 512)
    row = lax.broadcasted_iota(jnp.int32, (48, 128), 0)
    own_z = pick((row & 15) * 24 + z * 3 + (row >> 4), 512)
    xz[...] = dot(own_z, xb)

    remote(stat.at[pl.ds(1, 15)], stat.at[pl.ds(1, 15)], stat_s.at[0], stat_r, partners[0]).wait_recv()
    total = stat[0]
    for o in range(1, 16):
        total = total + stat[o]
    total = total * (1.0 / D)
    mean, square = total[0:1], total[1:2]
    scale = lax.rsqrt(square - mean * mean + 1e-06)
    mean_t = jnp.transpose(jnp.broadcast_to(mean, (128, 512)))
    scale_t = jnp.transpose(jnp.broadcast_to(scale, (128, 512)))
    gain = gain_ref[...]
    normed = jnp.concatenate(
        [
            ((xf[:, j * 128:(j + 1) * 128] - mean_t) * scale_t * gain[:, j * 128:(j + 1) * 128]).astype(BF16)
            for j in range(3)
        ],
        axis=1,
    )
    for b in range(8):
        place = relative(b)
        for g in range(4):
            a[g, place] = normed[g * 128 + b * 16:g * 128 + b * 16 + 16]
    for k in range(3):
        a[4 + k] = dot(chosen[k * 128:(k + 1) * 128], normed).astype(BF16).reshape(8, 16, 384)

    def offset(t):
        return 16 - (16 >> t)

    def rs_copy(u, c, t):
        at = pl.ds(offset(t), 8 >> t)
        return remote(snd.at[u, at], rcv.at[u, at], rs_s.at[u, t], rs_r.at[u, t], partners[(c + t) % 4])

    def place_of(c, b, h):
        own = ((b >> 2) & 1, (b >> 1) & 1, b & 1, h)
        return sum(own[(c + t) % 4] << (3 - t) for t in range(4))

    loaded = set()

    def product(u, rows, w, c):
        left = a[rows].reshape(128, 384)
        for h in range(2):
            if (w, h) not in loaded:
                load_wv[w, h].wait()
                loaded.add((w, h))
            value = dot(left, wv[w, h])
            for b in range(8):
                j = place_of(c, b, h)
                part = value[b * 16:(b + 1) * 16]
                if j >= 8:
                    snd[u, j - 8] = part.astype(BF16)
                else:
                    acc[u, j] = part
        start(rs_copy(u, c, 0))

    def rs_step(u, c, t):
        rs_copy(u, c, t - 1).wait_recv()
        half, at, to = 4 >> (t - 1), offset(t - 1), offset(t)
        snd[u, pl.ds(to, half)] = (
            acc[u, pl.ds(half, half)] + rcv[u, pl.ds(at + half, half)].astype(F32)
        ).astype(BF16)
        start(rs_copy(u, c, t))
        acc[u, pl.ds(0, half)] = acc[u, pl.ds(0, half)] + rcv[u, pl.ds(at, half)].astype(F32)

    def rs_last(u, c):
        rs_copy(u, c, 3).wait_recv()
        return acc[u, 0] + rcv[u, 14].astype(F32)

    head_gain = qkg_ref[:, half_at(0, vy)]

    def head_norm(value, which):
        parts = []
        for h in range(3):
            cut = slice(h * HD, (h + 1) * HD)
            v = value[:, cut]
            mean = jnp.mean(v, -1, keepdims=True)
            square = jnp.mean(v * v, -1, keepdims=True)
            parts.append((v - mean) * lax.rsqrt(square - mean * mean + 1e-06) * head_gain[which:which + 1, cut])
        return jnp.concatenate(parts, axis=1).astype(BF16)

    def kv_copy(c, s):
        n = 1 << s
        return remote(
            kv.at[c, pl.ds(0, n)], kv.at[c, pl.ds(n, n)], kv_s.at[c, s], kv_r.at[c, s], partners[(c + s) % 3]
        )

    def ag_copy(k, i, s):
        n, c = 1 << s, (i if i < 4 else k)
        return remote(
            agb.at[k, i, pl.ds(0, n)], agb.at[k, i, pl.ds(n, n)], ag_s.at[k, i, s], ag_r.at[k, i, s],
            partners[(c + 3 - s) % 4],
        )

    def ag_step(k, i, s):
        if s > 0:
            ag_copy(k, i, s - 1).wait_recv()
        if s < 4:
            start(ag_copy(k, i, s))

    def k_last(c):
        kv[c, 0, pl.ds(0, 16)] = head_norm(rs_last(K0 + c, c), 1)

    def v_last(c):
        kv[c, 0, pl.ds(16, 16)] = rs_last(V0 + c, c).astype(BF16)
        start(kv_copy(c, 0))

    def q_last(c):
        qn[c] = head_norm(rs_last(Q0 + c, c), 0)

    def m_last(k, c):
        value = rs_last(M0 + 4 * k + c, c)
        agb[k, c, 0] = (0.5 * value * (1.0 + lax.erf(value * (0.5 ** 0.5)))).astype(BF16)
        ag_step(k, c, 0)

    def kv_step(c, s):
        kv_copy(c, s - 1).wait_recv()
        if s < 3:
            start(kv_copy(c, s))

    def attention():
        row = lax.broadcasted_iota(jnp.int32, (48, HD), 0)
        first = (row & 15) * 24 + drow * 3 + (row >> 4) < c0
        queries = qn[...].reshape(48, 384)
        for h in range(3):
            cut = slice(h * HD, (h + 1) * HD)
            found = []
            for image in range(2):
                held = kv[pl.ds(2 * image, 2), :, :, cut]
                keys = held[:, :, 0:16].reshape(256, HD)
                values = held[:, :, 16:32].reshape(256, HD)
                scores = dot_t(queries[:, cut], keys) * HD ** (-0.5)
                expo = jnp.exp(scores - jnp.max(scores, -1, keepdims=True))
                weights = (expo / jnp.sum(expo, -1, keepdims=True)).astype(BF16)
                found.append(dot(weights, values))
            attended = jnp.where(first, found[0], found[1]).astype(BF16)
            for k in range(3):
                agb[k, 4, 0, :, cut] = attended[k * 16:(k + 1) * 16]
        for k in range(3):
            ag_step(k, 4, 0)

    def branch(k):
        value = None
        for i in range(5):
            c = i if i < 4 else k
            for h in range(2):
                left = jnp.concatenate([agb[k, i, place_of(c, b, h)] for b in range(8)], axis=0)
                if k == 0:
                    load_wd[i, h].wait()
                part = dot(left, wd[i, h])
                value = part if value is None else value + part
        bsum[k] = value.reshape(8, 16, 384)
        zs[k] = value.astype(BF16).reshape(8, 16, 384)
        for o in range(7):
            src = zs.at[k, relative(column[o])]
            start(remote(src, zr.at[k, o], z_s.at[k, o], z_r.at[k], (dp, mx, column[o])))

    def adapt(k):
        remote(zr.at[k], zr.at[k], z_s.at[k, 0], z_r.at[k], (dp, mx, column[0])).wait_recv()
        value = bsum[k, relative(z)]
        for o in range(7):
            value = value + zr[k, o].astype(F32)
        updated = (xz[pl.ds(k * 16, 16)] + value).astype(BF16)
        for b in range(8):
            part = dot(updated, wa[b])
            for j in range(4):
                tr[k, pl.ds(b * 4 + j, 16, stride=32), :] = part[:, j * 128:(j + 1) * 128]
        fs[k] = tr[k].astype(BF16).reshape(16, 32, 128)
        for o in range(15):
            start(remote(fs.at[k, plane[o]], fr.at[k, o], f_s.at[k, o], f_r.at[k], (dp, plane[o], z)))

    def finish(k):
        remote(fr.at[k], fr.at[k], f_s.at[k, 0], f_r.at[k], (dp, plane[0], z)).wait_recv()
        value = tr[k, pl.ds(pl.multiple_of(mx * 32, 32), 32)]
        for o in range(15):
            value = value + fr[k, o].astype(F32)
        out_ref[k] = value.astype(BF16)

    def adapter_across():
        load_wa.wait()
        some = wa.at[pl.ds(0, 7), pl.ds(0, 192)]
        remote(some, some, wz_s.at[0], wz_r, (dp, mx, column[0])).wait_recv()
        for o in range(7):
            at = wa.at[column[o], mine]
            start(remote(at, at, wc_s.at[o], wc_r, other))

    def adapter_ready():
        some = wa.at[pl.ds(0, 7), pl.ds(0, 192)]
        remote(some, some, wc_s.at[0], wc_r, other).wait_recv()

    four, three = range(4), range(3)

    def wave(first, count, t):
        for c in range(count):
            rs_step(first + c, c, t)

    def up(k):
        for c in four:
            product(M0 + 4 * k + c, 4 + k, 3 + c, c)

    def m_step(k, t):
        wave(M0 + 4 * k, 4, t)

    def m_end(k):
        for c in four:
            m_last(k, c)

    def gather(k, s):
        for c in four:
            ag_step(k, c, s)

    def gather_attended(s):
        for k in three:
            ag_step(k, 4, s)

    for c in four:
        product(K0 + c, c, 1, c)
    for c in four:
        product(V0 + c, c, 2, c)
    for c in three:
        product(Q0 + c, 4 + c, 0, c)
    wave(K0, 4, 1)
    wave(V0, 4, 1)
    up(0)
    wave(Q0, 3, 1)
    wave(K0, 4, 2)
    wave(V0, 4, 2)
    up(1)
    m_step(0, 1)
    wave(Q0, 3, 2)
    wave(K0, 4, 3)
    wave(V0, 4, 3)
    up(2)
    for c in four:
        k_last(c)
    for c in four:
        v_last(c)
    m_step(1, 1)
    m_step(0, 2)
    wave(Q0, 3, 3)
    for c in four:
        kv_step(c, 1)
    m_step(2, 1)
    m_step(1, 2)
    m_step(0, 3)
    for c in three:
        q_last(c)
    for c in four:
        kv_step(c, 2)
    m_step(2, 2)
    m_step(1, 3)
    m_end(0)
    for c in four:
        kv_step(c, 3)
    attention()
    m_step(2, 3)
    m_end(1)
    gather(0, 1)
    adapter_across()
    m_end(2)
    gather_attended(1)
    gather(0, 2)
    gather(1, 1)
    gather_attended(2)
    gather(0, 3)
    gather(1, 2)
    gather(2, 1)
    gather_attended(3)
    gather(1, 3)
    gather(2, 2)
    gather(0, 4)
    gather_attended(4)
    branch(0)
    gather(2, 3)
    gather(1, 4)
    branch(1)
    adapter_ready()
    adapt(0)
    gather(2, 4)
    branch(2)
    adapt(1)
    adapt(2)
    for k in three:
        finish(k)
    for copy in sent:
        copy.wait_send()


def per_device(patches, ln_gain, w_qkv, qk_gain, w_out, w_up, w_down, w_adapt, patch_counts):
    vmem, hbm = pl.BlockSpec(memory_space=pltpu.VMEM), pl.BlockSpec(memory_space=pl.ANY)
    dma = pltpu.SemaphoreType.DMA
    out = pl.pallas_call(
        kernel,
        out_shape=jax.ShapeDtypeStruct((3, 32, 128), BF16),
        in_specs=[hbm, vmem, hbm, vmem, hbm, hbm, hbm, hbm, pl.BlockSpec(memory_space=pltpu.SMEM)],
        out_specs=vmem,
        scratch_shapes=[
            pltpu.VMEM((512, 384), BF16),
            pltpu.VMEM((7, 8, 16, 384), BF16),
            pltpu.VMEM((7, 2, 384, 384), BF16),
            pltpu.VMEM((5, 2, 384, 384), BF16),
            pltpu.VMEM((8, 384, 512), BF16),
            pltpu.VMEM((16, 2, 512), F32),
            pltpu.VMEM((UNITS, 8, 16, 384), F32),
            pltpu.VMEM((UNITS, 15, 16, 384), BF16),
            pltpu.VMEM((UNITS, 15, 16, 384), BF16),
            pltpu.VMEM((4, 8, 32, 384), BF16),
            pltpu.VMEM((3, 16, 384), BF16),
            pltpu.VMEM((3, 5, 16, 16, 384), BF16),
            pltpu.VMEM((3, 8, 16, 384), BF16),
            pltpu.VMEM((3, 8, 16, 384), F32),
            pltpu.VMEM((3, 7, 16, 384), BF16),
            pltpu.VMEM((48, 384), F32),
            pltpu.VMEM((3, 512, 128), F32),
            pltpu.VMEM((3, 16, 32, 128), BF16),
            pltpu.VMEM((3, 15, 32, 128), BF16),
            dma, dma((7, 2)), dma((5, 2)), dma,
            dma((15,)), dma,
            dma((UNITS, 4)), dma((UNITS, 4)),
            dma((4, 3)), dma((4, 3)),
            dma((3, 5, 4)), dma((3, 5, 4)),
            dma((3, 7)), dma((3,)),
            dma((3, 15)), dma((3,)),
            dma((7,)), dma,
            dma((7,)), dma,
        ],
        compiler_params=pltpu.CompilerParams(
            collective_id=0, has_side_effects=True, vmem_limit_bytes=48 * 2**20
        ),
    )(patches, ln_gain.reshape(1, 384), w_qkv, qk_gain, w_out, w_up, w_down, w_adapt, patch_counts)
    return out.reshape(3, 4096)


def solution(mesh):
    return jax.shard_map(
        per_device,
        mesh=mesh,
        in_specs=(
            P("dp", "mx"),
            P("mx"),
            P(None, "mx", "my"),
            P(None, "my"),
            P("my", "mx"),
            P("mx", "my"),
            P("my", "mx"),
            P("mx", "my"),
            P("dp", None),
        ),
        out_specs=P(("dp", "mx", "my"), None),
        check_vma=False,
    )
```

time: 443 us -> 101 us (0.23)
  waiting for transfers between devices: 294 us -> 0 us
  Pallas kernels: 0 us -> 91.6 us
  blocking collectives: 52.6 us -> 0 us
  local copies, waits for them, and re-layouts: 39.6 us -> 8.86 us
  matrix products: 29.3 us -> 0 us
  other arithmetic: 14.7 us -> 0 us
  between operations: 13.3 us -> 0.02 us
    psum x3 -> x0, waiting for transfers between devices: 293 us -> none  [the longest x1 126 us: per_device(): lax.psum(lifted_part.astype(jnp.bfloat16), 'mx').astype(jnp.float32)]
    pallas_call x0 -> x1, Pallas kernels: none -> 91.6 us  [per_device(): pl.pallas_call(kernel, out_shape=jax.ShapeDtypeStruct((3, 32, 128), BF16)...]
    psum x1 -> x0, blocking collectives: 37.7 us -> none  [per_device(): lax.psum((jnp.sum(tokens_f, 1), jnp.sum(tokens_f * tokens_f, 1)), 'mx')]
    dot_general x7 -> x0, matrix products: 29.3 us -> none  [the longest x1 15.3 us: per_device(): jnp.dot(hidden, w_down, preferred_element_type=jnp.float32)]
    all_to_all x1 -> x0, blocking collectives: 14.8 us -> none  [per_device(): lax.all_to_all(routed, 'my', split_axis=0, concat_axis=2, tiled=True)]
    slice x5 -> x0, local copies, waits for them, and re-layouts: 10.8 us -> none  [the longest x2 6.37 us: finish(): projected[:, 0].reshape(count, heads, HD)]
    sub x4 -> x0, local copies, waits for them, and re-layouts: 8.85 us -> none  [row_norm(): return (values - mean) * lax.rsqrt(square - mean * mean + 1e-06) * gain]
    mul x4 -> x0, local copies, waits for them, and re-layouts: 8.81 us -> none  [row_norm(): return (values - mean) * lax.rsqrt(square - mean * mean + 1e-06) * gain]
  transfers between devices with their start and end apart: 3 -> 0, of which waited for: 3 -> 0; matrix products, arithmetic and copies ran while one was open for 0% -> 0% of each run, Pallas kernels for 0% -> 0%
where the time goes in v1:
time: 101 us
  Pallas kernels  91.6 us (91%)
  local copies, waits for them, and re-layouts  8.86 us (9%)
    pallas_call x1, Pallas kernels, per_device(): pl.pallas_call(kernel, out_shape=jax.ShapeDtypeStruct((3, 32, 128), BF16)...  91.6 us
    unnamed x15, local copies, waits for them, and re-layouts  8.17 us

profile of v1, /device:TPU:2, one launch (start us, length us, event | category | flops | bytes accessed | tf_op | source)
XLA Modules:
  0.0 100.5 jit_solution(7808521270627892223)
XLA Ops:
  0.0 0.7 reshape.6.gain_ref
  0.7 0.0 copy-start
  0.7 1.7 %copy-done = bf16[384,3072]{1,0:T(8,128)(2,1)S(1)} copy-done((bf16[384,3072]{1,0:T(8,128)(2,1)S(1)}, bf16[384,3072]{1,0:T(8,128)(2,1)}, u32[]{:S(2)}) %copy-start) | copy-done | bytes 2359320
  2.3 0.0 copy-start.1
  2.4 1.5 %copy-done.1 = bf16[3,384,768]{2,1,0:T(8,128)(2,1)S(1)} copy-done((bf16[3,384,768]{2,1,0:T(8,128)(2,1)S(1)}, bf16[3,384,768]{2,1,0:T(8,128)(2,1)}, u32[]{:S(2)}) %copy-start.1) | copy-done | bytes 1769496
  3.8 0.0 copy-start.2
  3.8 1.1 %copy-done.2 = bf16[768,384]{1,0:T(8,128)(2,1)S(1)} copy-done((bf16[768,384]{1,0:T(8,128)(2,1)S(1)}, bf16[768,384]{1,0:T(8,128)(2,1)}, u32[]{:S(2)}) %copy-start.2) | copy-done | bytes 589848
  4.9 0.0 copy-start.3
  4.9 1.0 copy-done.3
  5.9 0.0 copy-start.4
  5.9 1.0 copy-done.4
  6.9 0.0 copy-start.5
  6.9 0.7 copy-done.5
  7.6 0.0 copy-start.6
  7.6 0.7 copy-done.6
  8.2 91.6 %shard_map.91 = bf16[3,32,128]{2,1,0:T(8,128)(2,1)S(1)} custom-call(bf16[512,384]{1,0:T(8,128)(2,1)S(1)} %copy-done.3, f32[1,384]{1,0:T(1,128)S(1)} %reshape.6.gain_ref, bf16[3,384,768]{2,1,0:T(8,128)(2,1)S(1)} %copy-done.1, f32[2,768]{1,0:T(2,128)S(1)} %copy-done.5, bf16[768,384]{1,0:T(8,128)(2,1)S(1)} %copy-done.2, bf16[384,3072]{1,0:T(8,128)(2,1)S(1)} %copy-done, ...), custom_call_target="tpu_custom_call" | custom-call | tf_op jit(solution)/shard_map/pallas_call | solution.py:423
  99.9 0.6 copy.12
Async XLA Ops:
  0.7 1.7 %copy-start = (bf16[384,3072]{1,0:T(8,128)(2,1)S(1)}, bf16[384,3072]{1,0:T(8,128)(2,1)}, u32[]{:S(2)}) copy-start(bf16[384,3072]{1,0:T(8,128)(2,1)} %wup_hbm.1) | copy-start | bytes 7077892
  2.3 1.5 %copy-start.1 = (bf16[3,384,768]{2,1,0:T(8,128)(2,1)S(1)}, bf16[3,384,768]{2,1,0:T(8,128)(2,1)}, u32[]{:S(2)}) copy-start(bf16[3,384,768]{2,1,0:T(8,128)(2,1)} %wqkv_hbm.1) | copy-start | bytes 5308420
  3.8 1.1 %copy-start.2 = (bf16[768,384]{1,0:T(8,128)(2,1)S(1)}, bf16[768,384]{1,0:T(8,128)(2,1)}, u32[]{:S(2)}) copy-start(bf16[768,384]{1,0:T(8,128)(2,1)} %wout_hbm.1) | copy-start | bytes 1769476
  4.9 1.0 copy-start.3
  5.9 1.0 copy-start.4
  6.9 0.7 copy-start.5
  7.6 0.7 copy-start.6

commit v2 on v1

v2 whole, which is shorter than its diff:
```python
import jax
import jax.numpy as jnp
from jax import lax
from jax.experimental import pallas as pl
from jax.experimental.pallas import tpu as pltpu
from jax.sharding import PartitionSpec as P

MESH = pl.DeviceIdType.MESH
D = 6144
HD = 128
F32 = jnp.float32
BF16 = jnp.bfloat16

K0, V0, Q0, M0, UNITS = 0, 4, 8, 11, 23
Q_CLASS, A_CLASS = (3, 0, 2), (3, 1, 2)
UNIT = (
    [(c, 1, c) for c in range(4)]
    + [(c, 2, c) for c in range(4)]
    + [(4 + k, 0, Q_CLASS[k]) for k in range(3)]
    + [(4 + k, 3 + c, c) for k in range(3) for c in range(4)]
)
KV_LINKS = ((0, 1, 2), (1, 2, 0), (2, 0, 1), (2, 1, 0))
FIRST = (3, 0, 1, 2)

ORDER = (
    ("ch",), ("x",), ("greet",), ("p", 6), ("s", 0), ("c", 0), ("p", 5), ("p", 2), ("p", 7), ("p", 4), ("s", 1),
    ("w", 0), ("p", 1), ("p", 17), ("p", 3), ("r", 6, 1), ("c", 1), ("p", 0), ("p", 12), ("p", 13), ("r", 5, 1),
    ("r", 2, 1), ("p", 15), ("r", 7, 1), ("r", 4, 1), ("s", 2), ("c", 2), ("p", 8), ("r", 1, 1), ("r", 17, 1),
    ("r", 3, 1), ("w", 1), ("p", 21), ("r", 0, 1), ("r", 6, 2), ("r", 12, 1), ("r", 13, 1), ("p", 20), ("r", 2, 2),
    ("r", 4, 2), ("r", 5, 2), ("s", 3), ("p", 9), ("r", 15, 1), ("p", 22), ("r", 1, 2), ("c", 3), ("r", 7, 2),
    ("r", 8, 1), ("r", 0, 2), ("r", 3, 2), ("r", 17, 2), ("r", 6, 3), ("r", 21, 1), ("r", 2, 3), ("r", 13, 2),
    ("p", 16), ("r", 5, 3), ("r", 12, 2), ("r", 20, 1), ("w", 2), ("p", 19), ("r", 4, 3), ("p", 18), ("s", 4),
    ("r", 15, 2), ("r", 9, 1), ("r", 7, 3), ("r", 22, 1), ("r", 3, 3), ("r", 8, 2), ("r", 1, 3), ("p", 10),
    ("r", 17, 3), ("p", 14), ("c", 4), ("n",), ("r", 16, 1), ("r", 0, 3), ("p", 11), ("e", 6), ("r", 15, 3), ("e", 5),
    ("r", 19, 1), ("r", 20, 2), ("e", 7), ("e", 3), ("v", 3, 0), ("r", 9, 2), ("e", 4), ("e", 2), ("v", 2, 0),
    ("r", 21, 2), ("r", 18, 1), ("e", 1), ("v", 1, 0), ("r", 22, 2), ("r", 8, 3), ("r", 12, 3), ("r", 13, 3),
    ("e", 17), ("w", 3), ("r", 10, 1), ("r", 14, 1), ("e", 0), ("v", 0, 0), ("e", 15), ("r", 16, 2), ("r", 19, 2),
    ("r", 20, 3), ("v", 3, 1), ("r", 11, 1), ("r", 9, 3), ("v", 1, 1), ("r", 21, 3), ("v", 2, 1), ("r", 22, 3),
    ("e", 8), ("e", 13), ("g", 1, 2, 1), ("r", 18, 2), ("e", 12), ("r", 10, 2), ("g", 1, 0, 1), ("r", 19, 3),
    ("r", 16, 3), ("r", 14, 2), ("e", 9), ("v", 3, 2), ("v", 0, 1), ("e", 20), ("v", 1, 2), ("e", 22), ("r", 11, 2),
    ("e", 21), ("v", 2, 2), ("g", 0, 2, 1), ("w", 4), ("g", 1, 0, 2), ("e", 19), ("r", 18, 3), ("g", 1, 2, 2),
    ("g", 0, 1, 1), ("r", 14, 3), ("r", 10, 3), ("e", 16), ("v", 0, 2), ("g", 2, 3, 1), ("g", 2, 2, 1), ("r", 11, 3),
    ("g", 2, 0, 1), ("e", 18), ("v", 3, 3), ("e", 14), ("g", 2, 1, 1), ("g", 1, 2, 3), ("v", 2, 3), ("g", 0, 1, 2),
    ("e", 11), ("g", 1, 0, 3), ("v", 1, 3), ("e", 10), ("g", 0, 2, 2), ("g", 2, 3, 2), ("v", 0, 3), ("att",),
    ("g", 1, 1, 1), ("g", 1, 3, 1), ("g", 0, 0, 1), ("g", 0, 3, 1), ("g", 2, 1, 2), ("g", 2, 0, 2), ("g", 2, 2, 2),
    ("b", 1, 2), ("g", 0, 2, 3), ("b", 1, 0), ("g", 0, 1, 3), ("g", 2, 4, 1), ("g", 0, 4, 1), ("g", 2, 3, 3),
    ("g", 1, 1, 2), ("g", 1, 4, 1), ("g", 0, 0, 2), ("g", 1, 3, 2), ("g", 0, 3, 2), ("g", 2, 2, 3), ("g", 2, 1, 3),
    ("g", 2, 0, 3), ("g", 2, 4, 2), ("b", 0, 2), ("g", 1, 3, 3), ("b", 0, 1), ("b", 2, 3), ("g", 0, 4, 2),
    ("g", 1, 1, 3), ("g", 0, 3, 3), ("g", 1, 4, 2), ("g", 0, 0, 3), ("g", 2, 4, 3), ("b", 2, 2), ("b", 2, 0),
    ("b", 2, 1), ("g", 0, 4, 3), ("b", 1, 3), ("g", 1, 4, 3), ("b", 1, 1), ("b", 0, 0), ("b", 0, 3), ("b", 2, 4),
    ("z", 2), ("b", 0, 4), ("z", 0), ("b", 1, 4), ("z", 1), ("a", 2), ("a", 0), ("d",), ("a", 1), ("f", 2), ("f", 0),
    ("f", 1),
)


def dot(a, b):
    return jnp.dot(a, b, preferred_element_type=F32)


def dot_t(a, b):
    return lax.dot_general(a, b, (((1,), (1,)), ((), ())), preferred_element_type=F32)


def kernel(
    x_hbm, gain_ref, wqkv_hbm, qkg_ref, wout_hbm, wup_hbm, wdown_hbm, wad_hbm, cnt_ref,
    out_ref,
    x, a, wv, wd, wa, stat, cpk, cr, tt, corr, rst, acc, snd, rcv, kv, qn, agb, zs, bsum, zr, xz, tr, fs, fr,
    sem_x, sem_wv, sem_wd, sem_wa,
    stat_s, stat_r, c_s, c_r, rs_s, rs_r, kv_s, kv_r, ag_s, ag_r, z_s, z_r, f_s, f_r, wz_s, wz_r, wc_s, wc_r,
):
    dp, mx, z = lax.axis_index("dp"), lax.axis_index("mx"), lax.axis_index("my")
    cy, cx = mx // 4, mx % 4
    vx, vy = cx // 2, cy // 2
    ux = cx % 2 + vx - 2 * (cx % 2) * vx
    uy = cy % 2 + vy - 2 * (cy % 2) * vy
    bits = (ux, uy, vx, vy)
    drow = ux * 4 + uy * 2 + vx
    halves = (vy, 1 - vy)

    def flip(c):
        return c + 1 - 2 * (c % 2)

    partners = (
        (dp, cy * 4 + flip(cx), z),
        (dp, flip(cy) * 4 + cx, z),
        (dp, cy * 4 + 3 - cx, z),
        (dp, (3 - cy) * 4 + cx, z),
    )
    plane = [((cy + o // 4) % 4) * 4 + (cx + o % 4) % 4 for o in range(1, 16)]
    column = [(z + o) % 8 for o in range(1, 8)]
    other = (1 - dp, mx, z)

    def relative(block):
        total = 0
        for bit, weight in ((block // 4, 4), ((block // 2) % 2, 2), (block % 2, 1)):
            own = bits[{4: 0, 2: 1, 1: 2}[weight]]
            total = total + weight * (bit + own - 2 * bit * own)
        return total

    sent = []

    def remote(src, dst, s, r, device):
        return pltpu.make_async_remote_copy(
            src_ref=src, dst_ref=dst, send_sem=s, recv_sem=r, device_id=device, device_id_type=MESH
        )

    def start(copy):
        copy.start()
        sent.append(copy)

    barrier = pltpu.get_barrier_semaphore()
    for device in partners + ((dp, mx, column[0]), (dp, mx, column[6]), other):
        pl.semaphore_signal(barrier, inc=1, device_id=device, device_id_type=MESH)

    load_x = pltpu.make_async_copy(x_hbm, x, sem_x)
    load_x.start()
    load_wv, load_wd = {}, {}

    def half_at(base, half):
        return pl.ds(pl.multiple_of(base + half * 384, 128), 384)

    for i in (1, 2, 0, 3, 4, 5, 6):
        for h in range(2):
            if i < 3:
                src = wqkv_hbm.at[i, :, half_at(0, halves[h])]
            else:
                src = wup_hbm.at[:, half_at((i - 3) * 768, halves[h])]
            load_wv[i, h] = pltpu.make_async_copy(src, wv.at[i, h], sem_wv.at[i, h])
            load_wv[i, h].start()
    load_wa = pltpu.make_async_copy(wad_hbm, wa.at[z], sem_wa)
    load_wa.start()
    for i in range(5):
        for h in range(2):
            src = wdown_hbm.at[half_at(i * 768, halves[h])] if i < 4 else wout_hbm.at[half_at(0, halves[h])]
            load_wd[i, h] = pltpu.make_async_copy(src, wd.at[i, h], sem_wd.at[i, h])
            load_wd[i, h].start()

    mine = pl.ds(pl.multiple_of(dp * 192, 16), 192)

    def ring_copy(way, s):
        block, to = ((z + 8 - s) % 8, (z + 1) % 8) if way == 0 else ((z + s) % 8, (z + 7) % 8)
        src = wad_hbm.at[mine] if s == 0 else wa.at[block, mine]
        i = way * 4 + s
        return remote(src, wa.at[block, mine], wz_s.at[i], wz_r.at[i], (dp, mx, to))

    def across_copy(way, s):
        block = (z + 8 - s) % 8 if way == 0 else (z + s) % 8
        i = way * 4 + s - 1
        return remote(wa.at[block, mine], wa.at[block, mine], wc_s.at[i], wc_r.at[i], other)

    def ring_step(s):
        for way in range(2):
            steps = 4 - way
            if 0 < s <= steps:
                ring_copy(way, s - 1).wait_recv()
            if s < steps:
                start(ring_copy(way, s))
            if 0 < s <= steps:
                start(across_copy(way, s))

    load_x.wait()
    xb = x[...]
    xf = xb.astype(F32)
    gain = gain_ref[...]
    centred = ((xf - jnp.mean(xf, -1, keepdims=True)) * gain).astype(BF16)
    for b in range(8):
        place = relative(b)
        for g in range(4):
            a[g, place] = centred[g * 128 + b * 16:g * 128 + b * 16 + 16]

    c0 = cnt_ref[0, 0]

    def pick(slot):
        token = slot + jnp.where(slot >= c0, 256 - c0, 0)
        lane = lax.broadcasted_iota(jnp.int32, token.shape, 1)
        return jnp.concatenate([jnp.where(token == lane + 128 * j, 1.0, 0.0).astype(BF16) for j in range(4)], axis=1)

    def choose():
        row = lax.broadcasted_iota(jnp.int32, (384, 128), 0)
        block = jnp.bitwise_xor((row >> 4) & 7, drow)
        chosen = pick((row & 15) * 24 + block * 3 + (row >> 7))
        for k in range(3):
            a[4 + k] = dot(chosen[k * 128:(k + 1) * 128], centred).astype(BF16).reshape(8, 16, 384)

    loaded = set()

    def weights(w, h):
        if (w, h) not in loaded:
            load_wv[w, h].wait()
            loaded.add((w, h))
        return wv[w, h]

    def stat_copy(s):
        n = 1 << s
        return remote(stat.at[pl.ds(0, n)], stat.at[pl.ds(n, n)], stat_s.at[s], stat_r.at[s], partners[FIRST[s]])

    def stat_step(s):
        if s == 0:
            row8 = lax.broadcasted_iota(jnp.int32, (8, 384), 0)
            e0, e1 = (row8 == 0).astype(F32).astype(BF16), (row8 == 1).astype(F32).astype(BF16)
            x2 = xf * xf
            hi = x2.astype(BF16)
            lo = (x2 - hi.astype(F32)).astype(BF16)
            stat[0] = (dot_t(e0, xb) + dot_t(e1, hi) + dot_t(e1, lo))[0:2]
        else:
            stat_copy(s - 1).wait_recv()
        if s < 4:
            start(stat_copy(s))

    def split(value):
        hi = value.astype(BF16).astype(F32)
        return hi, (value - hi).astype(BF16).astype(F32)

    def c_copy(s):
        if s == 0:
            src, dst = cpk, cr.at[1]
        else:
            n = 1 << s
            src, dst = cr.at[pl.ds(0, n)], cr.at[pl.ds(n, n)]
        return remote(src, dst, c_s.at[s], c_r.at[s], partners[FIRST[s]])

    def c_step(s):
        if s == 0:
            g0, rest = split(gain)
            g1, g2 = split(gain - g0)
            row24 = lax.broadcasted_iota(jnp.int32, (24, 384), 0)
            parts = jnp.where(row24 < 8, g0, jnp.where(row24 < 16, g1, g2))
            for h in (1, 0):
                value = None
                for w in range(7):
                    left = jnp.where((row24 & 7) == w, parts, 0.0).astype(BF16)
                    part = dot(left, weights(w, h))
                    value = part if value is None else value + part
                sums = jnp.concatenate(split(value[0:8] + value[8:16] + value[16:24]), axis=0).astype(BF16)
                if h == 1:
                    cpk[...] = sums
                else:
                    cr[0] = sums
        else:
            c_copy(s - 1).wait_recv()
        if s < 4:
            start(c_copy(s))

    def correct():
        sums = jnp.concatenate([stat[j][0:1] for j in range(16)], axis=0)
        squares = jnp.concatenate([stat[j][1:2] for j in range(16)], axis=0)
        mean = jnp.sum(sums, 0, keepdims=True) * (1.0 / D)
        square = jnp.sum(squares, 0, keepdims=True) * (1.0 / D)
        scale = lax.rsqrt(square - mean * mean + 1e-06)
        hi, lo = split(sums * (1.0 / 384) - mean)
        s0, rest = split(scale)
        s1, s2 = split(scale - s0)
        row8 = lax.broadcasted_iota(jnp.int32, (8, 512), 0)
        scales = jnp.where(row8 == 0, s0, jnp.where(row8 == 1, s1, jnp.where(row8 == 2, s2, 0.0)))
        table = jnp.concatenate([hi, lo, scales, jnp.zeros((88, 512), F32)], axis=0)
        table = jnp.transpose(table).astype(BF16)
        tt[...] = table.reshape(4, 8, 16, 128)
        row = lax.broadcasted_iota(jnp.int32, (48, 128), 0)
        own = dot(pick((row & 15) * 24 + drow * 3 + (row >> 4)), table).astype(BF16)
        rows = [tt[r, drow] if r < 4 else own[(r - 4) * 16:(r - 3) * 16] for r, w, c in UNIT]
        left = jnp.concatenate(rows, axis=0)
        j = lax.broadcasted_iota(jnp.int32, (128, 256), 0)
        lane = lax.broadcasted_iota(jnp.int32, (128, 256), 1)
        spread_hi = jnp.where((lane >> 4) == j, 1.0, 0.0).astype(BF16)
        spread_lo = jnp.where((lane >> 4) + 16 == j, 1.0, 0.0).astype(BF16)
        j = lax.broadcasted_iota(jnp.int32, (128, 128), 0)
        spread_scale = jnp.where((j >= 32) & (j < 35), 1.0, 0.0).astype(BF16)
        rst[...] = dot(left, spread_scale).reshape(UNITS, 16, 128)
        unit = lax.broadcasted_iota(jnp.int32, (UNITS * 16, 256), 0) >> 4
        group = jnp.where(unit < V0, 1, jnp.where(unit < Q0, 2, jnp.where(unit < M0, 0, 3 + ((unit - M0) & 3))))
        at = lax.broadcasted_iota(jnp.int32, (UNITS * 16, 256), 1) & 15
        left_hi = jnp.where((at & 7) == group, dot(left, spread_hi), 0.0).astype(BF16)
        left_lo = jnp.where(at == group, dot(left, spread_lo), 0.0).astype(BF16)
        held = cr[...].reshape(256, 384)
        corr[...] = (dot(left_hi, held) + dot(left_lo, held)).reshape(UNITS, 16, 384)

    def offset(t):
        return 16 - (16 >> t)

    def rs_copy(u, c, t):
        at = pl.ds(offset(t), 8 >> t)
        return remote(snd.at[u, at], rcv.at[u, at], rs_s.at[u, t], rs_r.at[u, t], partners[(c + t) % 4])

    def place_of(c, b, h):
        own = ((b >> 2) & 1, (b >> 1) & 1, b & 1, h)
        return sum(own[(c + t) % 4] << (3 - t) for t in range(4))

    def product(u):
        rows, w, c = UNIT[u]
        left = a[rows].reshape(128, 384)
        for h in range(2):
            value = dot(left, weights(w, h))
            for b in range(8):
                j = place_of(c, b, h)
                part = value[b * 16:(b + 1) * 16]
                if j >= 8:
                    snd[u, j - 8] = part.astype(BF16)
                else:
                    acc[u, j] = part
        start(rs_copy(u, c, 0))

    def rs_step(u, t):
        c = UNIT[u][2]
        rs_copy(u, c, t - 1).wait_recv()
        half, at, to = 4 >> (t - 1), offset(t - 1), offset(t)
        snd[u, pl.ds(to, half)] = (
            acc[u, pl.ds(half, half)] + rcv[u, pl.ds(at + half, half)].astype(F32)
        ).astype(BF16)
        start(rs_copy(u, c, t))
        acc[u, pl.ds(0, half)] = acc[u, pl.ds(0, half)] + rcv[u, pl.ds(at, half)].astype(F32)

    def rs_last(u):
        rs_copy(u, UNIT[u][2], 3).wait_recv()
        value = acc[u, 0] + rcv[u, 14].astype(F32) + corr[u]
        return value * jnp.concatenate([rst[u]] * 3, axis=1)

    head_gain = qkg_ref[:, half_at(0, vy)]

    def head_norm(value, which):
        parts = []
        for h in range(3):
            cut = slice(h * HD, (h + 1) * HD)
            v = value[:, cut]
            mean = jnp.mean(v, -1, keepdims=True)
            square = jnp.mean(v * v, -1, keepdims=True)
            parts.append((v - mean) * lax.rsqrt(square - mean * mean + 1e-06) * head_gain[which:which + 1, cut])
        return jnp.concatenate(parts, axis=1).astype(BF16)

    def kv_copy(c, s):
        n = 1 << s
        return remote(
            kv.at[c, pl.ds(0, n)], kv.at[c, pl.ds(n, n)], kv_s.at[c, s], kv_r.at[c, s], partners[KV_LINKS[c][s]]
        )

    def ag_copy(k, i, s):
        n, c = 1 << s, (i if i < 4 else A_CLASS[k])
        return remote(
            agb.at[k, i, pl.ds(0, n)], agb.at[k, i, pl.ds(n, n)], ag_s.at[k, i, s], ag_r.at[k, i, s],
            partners[(c + 3 - s) % 4],
        )

    def ag_step(k, i, s):
        if s > 0:
            ag_copy(k, i, s - 1).wait_recv()
        if s < 4:
            start(ag_copy(k, i, s))

    def rs_end(u):
        value = rs_last(u)
        if u < V0:
            kv[u, 0, pl.ds(0, 16)] = head_norm(value, 1)
        elif u < Q0:
            kv[u - V0, 0, pl.ds(16, 16)] = value.astype(BF16)
        elif u < M0:
            qn[u - Q0] = head_norm(value, 0)
        else:
            k, c = (u - M0) // 4, (u - M0) % 4
            agb[k, c, 0] = (0.5 * value * (1.0 + lax.erf(value * (0.5 ** 0.5)))).astype(BF16)
            ag_step(k, c, 0)

    def kv_step(c, s):
        if s > 0:
            kv_copy(c, s - 1).wait_recv()
        if s < 3:
            start(kv_copy(c, s))

    def attention():
        row = lax.broadcasted_iota(jnp.int32, (48, HD), 0)
        first = (row & 15) * 24 + drow * 3 + (row >> 4) < c0
        queries = qn[...].reshape(48, 384)
        for h in range(3):
            cut = slice(h * HD, (h + 1) * HD)
            found = []
            for image in range(2):
                held = kv[pl.ds(2 * image, 2), :, :, cut]
                keys = held[:, :, 0:16].reshape(256, HD)
                values = held[:, :, 16:32].reshape(256, HD)
                scores = dot_t(queries[:, cut], keys) * HD ** (-0.5)
                expo = jnp.exp(scores - jnp.max(scores, -1, keepdims=True))
                weights = (expo / jnp.sum(expo, -1, keepdims=True)).astype(BF16)
                found.append(dot(weights, values))
            attended = jnp.where(first, found[0], found[1]).astype(BF16)
            for k in range(3):
                agb[k, 4, 0, :, cut] = attended[k * 16:(k + 1) * 16]
        for k in range(3):
            ag_step(k, 4, 0)

    begun, loaded_wd = set(), set()

    def branch(k, i):
        ag_step(k, i, 4)
        c = i if i < 4 else A_CLASS[k]
        value = None
        for h in range(2):
            left = jnp.concatenate([agb[k, i, place_of(c, b, h)] for b in range(8)], axis=0)
            if (i, h) not in loaded_wd:
                load_wd[i, h].wait()
                loaded_wd.add((i, h))
            part = dot(left, wd[i, h])
            value = part if value is None else value + part
        value = value.reshape(8, 16, 384)
        bsum[k] = bsum[k] + value if k in begun else value
        begun.add(k)

    def z_send(k):
        zs[k] = bsum[k].astype(BF16)
        for o in range(7):
            src = zs.at[k, relative(column[o])]
            start(remote(src, zr.at[k, o], z_s.at[k, o], z_r.at[k], (dp, mx, column[o])))

    def adapt(k):
        if not begun & {"a"}:
            adapter_ready()
            begun.add("a")
        remote(zr.at[k], zr.at[k], z_s.at[k, 0], z_r.at[k], (dp, mx, column[0])).wait_recv()
        value = bsum[k, relative(z)]
        for o in range(7):
            value = value + zr[k, o].astype(F32)
        updated = (xz[pl.ds(k * 16, 16)] + value).astype(BF16)
        for b in range(8):
            part = dot(updated, wa[b])
            for j in range(4):
                tr[k, pl.ds(b * 4 + j, 16, stride=32), :] = part[:, j * 128:(j + 1) * 128]
        fs[k] = tr[k].astype(BF16).reshape(16, 32, 128)
        for o in range(15):
            start(remote(fs.at[k, plane[o]], fr.at[k, o], f_s.at[k, o], f_r.at[k], (dp, plane[o], z)))

    def finish(k):
        remote(fr.at[k], fr.at[k], f_s.at[k, 0], f_r.at[k], (dp, plane[0], z)).wait_recv()
        value = tr[k, pl.ds(pl.multiple_of(mx * 32, 32), 32)]
        for o in range(15):
            value = value + fr[k, o].astype(F32)
        out_ref[k] = value.astype(BF16)

    def adapter_ready():
        load_wa.wait()
        for way in range(2):
            for s in range(1, 5 - way):
                across_copy(way, s).wait_recv()

    def residual():
        row = lax.broadcasted_iota(jnp.int32, (48, 128), 0)
        xz[...] = dot(pick((row & 15) * 24 + z * 3 + (row >> 4)), xb)

    def drain():
        while sent:
            sent.pop(0).wait_send()

    def greet():
        pl.semaphore_wait(barrier, 7)

    events = {
        "greet": greet, "p": product, "r": rs_step, "e": rs_end, "v": kv_step, "att": attention, "g": ag_step,
        "b": branch, "z": z_send, "a": adapt, "f": finish, "w": ring_step, "s": stat_step, "c": c_step,
        "n": correct, "d": drain, "x": residual, "ch": choose,
    }
    for event in ORDER:
        events[event[0]](*event[1:])
    drain()


def per_device(patches, ln_gain, w_qkv, qk_gain, w_out, w_up, w_down, w_adapt, patch_counts):
    vmem, hbm = pl.BlockSpec(memory_space=pltpu.VMEM), pl.BlockSpec(memory_space=pl.ANY)
    dma = pltpu.SemaphoreType.DMA
    out = pl.pallas_call(
        kernel,
        out_shape=jax.ShapeDtypeStruct((3, 32, 128), BF16),
        in_specs=[hbm, vmem, hbm, vmem, hbm, hbm, hbm, hbm, pl.BlockSpec(memory_space=pltpu.SMEM)],
        out_specs=vmem,
        scratch_shapes=[
            pltpu.VMEM((512, 384), BF16),
            pltpu.VMEM((7, 8, 16, 384), BF16),
            pltpu.VMEM((7, 2, 384, 384), BF16),
            pltpu.VMEM((5, 2, 384, 384), BF16),
            pltpu.VMEM((8, 384, 512), BF16),
            pltpu.VMEM((16, 2, 512), F32),
            pltpu.VMEM((16, 384), BF16),
            pltpu.VMEM((16, 16, 384), BF16),
            pltpu.VMEM((4, 8, 16, 128), BF16),
            pltpu.VMEM((UNITS, 16, 384), F32),
            pltpu.VMEM((UNITS, 16, 128), F32),
            pltpu.VMEM((UNITS, 8, 16, 384), F32),
            pltpu.VMEM((UNITS, 15, 16, 384), BF16),
            pltpu.VMEM((UNITS, 15, 16, 384), BF16),
            pltpu.VMEM((4, 8, 32, 384), BF16),
            pltpu.VMEM((3, 16, 384), BF16),
            pltpu.VMEM((3, 5, 16, 16, 384), BF16),
            pltpu.VMEM((3, 8, 16, 384), BF16),
            pltpu.VMEM((3, 8, 16, 384), F32),
            pltpu.VMEM((3, 7, 16, 384), BF16),
            pltpu.VMEM((48, 384), F32),
            pltpu.VMEM((3, 512, 128), F32),
            pltpu.VMEM((3, 16, 32, 128), BF16),
            pltpu.VMEM((3, 15, 32, 128), BF16),
            dma, dma((7, 2)), dma((5, 2)), dma,
            dma((4,)), dma((4,)),
            dma((4,)), dma((4,)),
            dma((UNITS, 4)), dma((UNITS, 4)),
            dma((4, 3)), dma((4, 3)),
            dma((3, 5, 4)), dma((3, 5, 4)),
            dma((3, 7)), dma((3,)),
            dma((3, 15)), dma((3,)),
            dma((7,)), dma((7,)),
            dma((7,)), dma((7,)),
        ],
        compiler_params=pltpu.CompilerParams(
            collective_id=0, has_side_effects=True, vmem_limit_bytes=60 * 2**20
        ),
    )(patches, ln_gain.reshape(1, 384), w_qkv, qk_gain, w_out, w_up, w_down, w_adapt, patch_counts)
    return out.reshape(3, 4096)


def solution(mesh):
    return jax.shard_map(
        per_device,
        mesh=mesh,
        in_specs=(
            P("dp", "mx"),
            P("mx"),
            P(None, "mx", "my"),
            P(None, "my"),
            P("my", "mx"),
            P("mx", "my"),
            P("my", "mx"),
            P("mx", "my"),
            P("dp", None),
        ),
        out_specs=P(("dp", "mx", "my"), None),
        check_vma=False,
    )
```

time: 101 us -> 90.4 us (0.90)
  local copies, waits for them, and re-layouts: 8.86 us -> 2.61 us
  Pallas kernels: 91.6 us -> 86.4 us
    unnamed x15 -> x1, local copies, waits for them, and re-layouts: 8.17 us -> 1.37 us
    pallas_call x1, Pallas kernels: 91.6 us -> 86.4 us  [per_device(): pl.pallas_call(kernel, out_shape=jax.ShapeDtypeStruct((3, 32, 128), BF16)...]
where the time goes in v2:
time: 90.4 us; the launch traced here: 89.1 us
  Pallas kernels  86.4 us (96%)
  local copies, waits for them, and re-layouts  2.61 us (3%)
    pallas_call x1, Pallas kernels, per_device(): pl.pallas_call(kernel, out_shape=jax.ShapeDtypeStruct((3, 32, 128), BF16)...  86.4 us

profile of v2, /device:TPU:2, one launch (start us, length us, event | category | flops | bytes accessed | tf_op | source)
XLA Modules:
  0.0 89.1 jit_solution(15830520662257534724)
XLA Ops:
  0.0 1.2 %reshape.6.gain_ref = f32[1,384]{1,0:T(1,128)} reshape(f32[384]{0:T(512)} %param.10) | data formatting | bytes 3072 | tf_op jit(solution)/shard_map/reshape | solution.py:509
  1.2 86.4 %shard_map.91 = bf16[3,32,128]{2,1,0:T(8,128)(2,1)} custom-call(bf16[512,384]{1,0:T(8,128)(2,1)} %x_hbm.1, f32[1,384]{1,0:T(1,128)} %reshape.6.gain_ref, bf16[3,384,768]{2,1,0:T(8,128)(2,1)} %wqkv_hbm.1, f32[2,768]{1,0:T(2,128)} %qkg_ref.1, bf16[768,384]{1,0:T(8,128)(2,1)} %wout_hbm.1, bf16[384,3072]{1,0:T(8,128)(2,1)} %wup_hbm.1, ...), custom_call_target="tpu_custom_call" | custom-call | tf_op jit(solution)/shard_map/pallas_call | solution.py:465
  87.7 1.4 %copy.12 = bf16[1,3,32,128]{3,1,2,0:T(4,128)(2,1)} copy(bf16[1,3,32,128]{3,2,1,0:T(8,128)(2,1)} %bitcast.4) | data formatting | bytes 49152

commit v3 on v2

--- a/solution.py
+++ b/solution.py
@@ -11,45 +11,40 @@
 F32 = jnp.float32
 BF16 = jnp.bfloat16
 
-K0, V0, Q0, M0, UNITS = 0, 4, 8, 11, 23
+Q0, M0, UNITS = 4, 7, 19
 Q_CLASS, A_CLASS = (3, 0, 2), (3, 1, 2)
-UNIT = (
-    [(c, 1, c) for c in range(4)]
-    + [(c, 2, c) for c in range(4)]
-    + [(4 + k, 0, Q_CLASS[k]) for k in range(3)]
-    + [(4 + k, 3 + c, c) for k in range(3) for c in range(4)]
+CLASS = (0, 1, 2, 3) + Q_CLASS + (0, 1, 2, 3) * 3
+BLOCKS = (
+    [(c, 1) for c in range(4)]
+    + [(c, 2) for c in range(4)]
+    + [(4 + k, 0) for k in range(3)]
+    + [(4 + k, 3 + c) for k in range(3) for c in range(4)]
 )
 KV_LINKS = ((0, 1, 2), (1, 2, 0), (2, 0, 1), (2, 1, 0))
 FIRST = (3, 0, 1, 2)
 
 ORDER = (
-    ("ch",), ("x",), ("greet",), ("p", 6), ("s", 0), ("c", 0), ("p", 5), ("p", 2), ("p", 7), ("p", 4), ("s", 1),
-    ("w", 0), ("p", 1), ("p", 17), ("p", 3), ("r", 6, 1), ("c", 1), ("p", 0), ("p", 12), ("p", 13), ("r", 5, 1),
-    ("r", 2, 1), ("p", 15), ("r", 7, 1), ("r", 4, 1), ("s", 2), ("c", 2), ("p", 8), ("r", 1, 1), ("r", 17, 1),
-    ("r", 3, 1), ("w", 1), ("p", 21), ("r", 0, 1), ("r", 6, 2), ("r", 12, 1), ("r", 13, 1), ("p", 20), ("r", 2, 2),
-    ("r", 4, 2), ("r", 5, 2), ("s", 3), ("p", 9), ("r", 15, 1), ("p", 22), ("r", 1, 2), ("c", 3), ("r", 7, 2),
-    ("r", 8, 1), ("r", 0, 2), ("r", 3, 2), ("r", 17, 2), ("r", 6, 3), ("r", 21, 1), ("r", 2, 3), ("r", 13, 2),
-    ("p", 16), ("r", 5, 3), ("r", 12, 2), ("r", 20, 1), ("w", 2), ("p", 19), ("r", 4, 3), ("p", 18), ("s", 4),
-    ("r", 15, 2), ("r", 9, 1), ("r", 7, 3), ("r", 22, 1), ("r", 3, 3), ("r", 8, 2), ("r", 1, 3), ("p", 10),
-    ("r", 17, 3), ("p", 14), ("c", 4), ("n",), ("r", 16, 1), ("r", 0, 3), ("p", 11), ("e", 6), ("r", 15, 3), ("e", 5),
-    ("r", 19, 1), ("r", 20, 2), ("e", 7), ("e", 3), ("v", 3, 0), ("r", 9, 2), ("e", 4), ("e", 2), ("v", 2, 0),
-    ("r", 21, 2), ("r", 18, 1), ("e", 1), ("v", 1, 0), ("r", 22, 2), ("r", 8, 3), ("r", 12, 3), ("r", 13, 3),
-    ("e", 17), ("w", 3), ("r", 10, 1), ("r", 14, 1), ("e", 0), ("v", 0, 0), ("e", 15), ("r", 16, 2), ("r", 19, 2),
-    ("r", 20, 3), ("v", 3, 1), ("r", 11, 1), ("r", 9, 3), ("v", 1, 1), ("r", 21, 3), ("v", 2, 1), ("r", 22, 3),
-    ("e", 8), ("e", 13), ("g", 1, 2, 1), ("r", 18, 2), ("e", 12), ("r", 10, 2), ("g", 1, 0, 1), ("r", 19, 3),
-    ("r", 16, 3), ("r", 14, 2), ("e", 9), ("v", 3, 2), ("v", 0, 1), ("e", 20), ("v", 1, 2), ("e", 22), ("r", 11, 2),
-    ("e", 21), ("v", 2, 2), ("g", 0, 2, 1), ("w", 4), ("g", 1, 0, 2), ("e", 19), ("r", 18, 3), ("g", 1, 2, 2),
-    ("g", 0, 1, 1), ("r", 14, 3), ("r", 10, 3), ("e", 16), ("v", 0, 2), ("g", 2, 3, 1), ("g", 2, 2, 1), ("r", 11, 3),
-    ("g", 2, 0, 1), ("e", 18), ("v", 3, 3), ("e", 14), ("g", 2, 1, 1), ("g", 1, 2, 3), ("v", 2, 3), ("g", 0, 1, 2),
-    ("e", 11), ("g", 1, 0, 3), ("v", 1, 3), ("e", 10), ("g", 0, 2, 2), ("g", 2, 3, 2), ("v", 0, 3), ("att",),
-    ("g", 1, 1, 1), ("g", 1, 3, 1), ("g", 0, 0, 1), ("g", 0, 3, 1), ("g", 2, 1, 2), ("g", 2, 0, 2), ("g", 2, 2, 2),
-    ("b", 1, 2), ("g", 0, 2, 3), ("b", 1, 0), ("g", 0, 1, 3), ("g", 2, 4, 1), ("g", 0, 4, 1), ("g", 2, 3, 3),
-    ("g", 1, 1, 2), ("g", 1, 4, 1), ("g", 0, 0, 2), ("g", 1, 3, 2), ("g", 0, 3, 2), ("g", 2, 2, 3), ("g", 2, 1, 3),
-    ("g", 2, 0, 3), ("g", 2, 4, 2), ("b", 0, 2), ("g", 1, 3, 3), ("b", 0, 1), ("b", 2, 3), ("g", 0, 4, 2),
-    ("g", 1, 1, 3), ("g", 0, 3, 3), ("g", 1, 4, 2), ("g", 0, 0, 3), ("g", 2, 4, 3), ("b", 2, 2), ("b", 2, 0),
-    ("b", 2, 1), ("g", 0, 4, 3), ("b", 1, 3), ("g", 1, 4, 3), ("b", 1, 1), ("b", 0, 0), ("b", 0, 3), ("b", 2, 4),
-    ("z", 2), ("b", 0, 4), ("z", 0), ("b", 1, 4), ("z", 1), ("a", 2), ("a", 0), ("d",), ("a", 1), ("f", 2), ("f", 0),
-    ("f", 1),
+    ("ch",), ("x",), ("greet",), ("p", 18), ("p", 17), ("p", 16), ("p", 0), ("s", 0), ("p", 10), ("p", 12), ("p", 13),
+    ("c", 0), ("p", 2), ("p", 1), ("p", 7), ("p", 14), ("w", 0), ("r", 17, 1), ("r", 16, 1), ("s", 1), ("r", 18, 1),
+    ("p", 3), ("c", 1), ("r", 10, 1), ("r", 12, 1), ("r", 13, 1), ("r", 0, 1), ("p", 11), ("r", 14, 1), ("r", 7, 1),
+    ("p", 9), ("s", 2), ("r", 17, 2), ("r", 18, 2), ("r", 2, 1), ("r", 1, 1), ("c", 2), ("w", 1), ("r", 16, 2),
+    ("r", 10, 2), ("p", 15), ("r", 12, 2), ("p", 8), ("r", 0, 2), ("r", 3, 1), ("r", 7, 2), ("r", 11, 1), ("s", 3),
+    ("r", 9, 1), ("r", 18, 3), ("r", 13, 2), ("r", 14, 2), ("r", 17, 3), ("c", 3), ("r", 10, 3), ("p", 4), ("p", 5),
+    ("r", 1, 2), ("r", 16, 3), ("r", 15, 1), ("r", 2, 2), ("p", 6), ("r", 8, 1), ("r", 7, 3), ("r", 12, 3), ("w", 2),
+    ("s", 4), ("r", 11, 2), ("r", 3, 2), ("r", 9, 2), ("r", 14, 3), ("r", 13, 3), ("r", 15, 2), ("c", 4), ("n",),
+    ("e", 18), ("e", 17), ("r", 4, 1), ("e", 0), ("e", 1), ("e", 16), ("e", 13), ("e", 7), ("e", 2), ("r", 8, 2),
+    ("r", 11, 3), ("r", 9, 3), ("e", 12), ("g", 2, 2, 1), ("e", 10), ("r", 5, 1), ("e", 3), ("e", 14), ("r", 15, 3),
+    ("g", 0, 0, 1), ("g", 2, 3, 1), ("v", 0, 1), ("g", 2, 1, 1), ("g", 1, 2, 1), ("r", 6, 1), ("r", 4, 2),
+    ("r", 8, 3), ("e", 11), ("v", 1, 1), ("g", 1, 1, 1), ("e", 9), ("w", 3), ("g", 2, 2, 2), ("v", 2, 1), ("r", 5, 2),
+    ("e", 15), ("g", 0, 3, 1), ("g", 2, 1, 2), ("v", 3, 1), ("g", 1, 2, 2), ("g", 1, 3, 1), ("e", 8), ("g", 2, 3, 2),
+    ("g", 0, 0, 2), ("r", 6, 2), ("g", 1, 0, 1), ("g", 0, 2, 1), ("g", 1, 1, 2), ("v", 1, 2), ("g", 2, 2, 3),
+    ("v", 0, 2), ("e", 4), ("v", 2, 2), ("g", 2, 0, 1), ("e", 5), ("g", 0, 3, 2), ("g", 1, 3, 2), ("g", 1, 2, 3),
+    ("v", 3, 2), ("g", 2, 1, 3), ("g", 0, 1, 1), ("w", 4), ("g", 1, 0, 2), ("g", 0, 0, 3), ("g", 2, 3, 3),
+    ("g", 1, 1, 3), ("e", 6), ("att",), ("g", 0, 2, 2), ("g", 2, 0, 2), ("g", 0, 1, 2), ("g", 1, 3, 3), ("b", 2, 1),
+    ("g", 0, 3, 3), ("b", 2, 2), ("g", 1, 0, 3), ("b", 2, 3), ("b", 0, 0), ("b", 1, 2), ("g", 1, 4, 1), ("b", 1, 1),
+    ("g", 0, 2, 3), ("g", 0, 4, 1), ("g", 0, 1, 3), ("g", 2, 4, 1), ("g", 2, 0, 3), ("b", 1, 3), ("b", 1, 0),
+    ("b", 1, 4), ("z", 1), ("b", 0, 3), ("b", 0, 2), ("b", 0, 1), ("b", 0, 4), ("z", 0), ("b", 2, 0), ("b", 2, 4),
+    ("z", 2), ("a", 1), ("a", 0), ("d",), ("a", 2), ("f", 1), ("f", 0), ("f", 2),
 )
 
 
@@ -64,7 +59,7 @@
 def kernel(
     x_hbm, gain_ref, wqkv_hbm, qkg_ref, wout_hbm, wup_hbm, wdown_hbm, wad_hbm, cnt_ref,
     out_ref,
-    x, a, wv, wd, wa, stat, cpk, cr, tt, corr, rst, acc, snd, rcv, kv, qn, agb, zs, bsum, zr, xz, tr, fs, fr,
+    x, a, wv, wd, wa, stat, cpk, cr, tt, corr, rst, acc, snd, rcv, acc2, snd2, rcv2, kv, qn, agb, zs, bsum, zr, xz, tr, fs, fr,
     sem_x, sem_wv, sem_wd, sem_wa,
     stat_s, stat_r, c_s, c_r, rs_s, rs_r, kv_s, kv_r, ag_s, ag_r, z_s, z_r, f_s, f_r, wz_s, wz_r, wc_s, wc_r,
 ):
@@ -80,12 +75,20 @@
     def flip(c):
         return c + 1 - 2 * (c % 2)
 
-    partners = (
-        (dp, cy * 4 + flip(cx), z),
-        (dp, flip(cy) * 4 + cx, z),
-        (dp, cy * 4 + 3 - cx, z),
-        (dp, (3 - cy) * 4 + cx, z),
-    )
+    def towards(*dims):
+        py, px = cy, cx
+        for d in dims:
+            if d == 0:
+                px = flip(px)
+            elif d == 1:
+                py = flip(py)
+            elif d == 2:
+                px = 3 - px
+            else:
+                py = 3 - py
+        return (dp, py * 4 + px, z)
+
+    partners = tuple(towards(d) for d in range(4))
     plane = [((cy + o // 4) % 4) * 4 + (cx + o % 4) % 4 for o in range(1, 16)]
     column = [(z + o) % 8 for o in range(1, 8)]
     other = (1 - dp, mx, z)
@@ -139,9 +142,8 @@
 
     def ring_copy(way, s):
         block, to = ((z + 8 - s) % 8, (z + 1) % 8) if way == 0 else ((z + s) % 8, (z + 7) % 8)
-        src = wad_hbm.at[mine] if s == 0 else wa.at[block, mine]
         i = way * 4 + s
-        return remote(src, wa.at[block, mine], wz_s.at[i], wz_r.at[i], (dp, mx, to))
+        return remote(wa.at[block, mine], wa.at[block, mine], wz_s.at[i], wz_r.at[i], (dp, mx, to))
 
     def across_copy(way, s):
         block = (z + 8 - s) % 8 if way == 0 else (z + s) % 8
@@ -149,6 +151,8 @@
         return remote(wa.at[block, mine], wa.at[block, mine], wc_s.at[i], wc_r.at[i], other)
 
     def ring_step(s):
+        if s == 0:
+            load_wa.wait()
         for way in range(2):
             steps = 4 - way
             if 0 < s <= steps:
@@ -257,7 +261,7 @@
         tt[...] = table.reshape(4, 8, 16, 128)
         row = lax.broadcasted_iota(jnp.int32, (48, 128), 0)
         own = dot(pick((row & 15) * 24 + drow * 3 + (row >> 4)), table).astype(BF16)
-        rows = [tt[r, drow] if r < 4 else own[(r - 4) * 16:(r - 3) * 16] for r, w, c in UNIT]
+        rows = [tt[r, drow] if r < 4 else own[(r - 4) * 16:(r - 3) * 16] for r, w in BLOCKS]
         left = jnp.concatenate(rows, axis=0)
         j = lax.broadcasted_iota(jnp.int32, (128, 256), 0)
         lane = lax.broadcasted_iota(jnp.int32, (128, 256), 1)
@@ -265,54 +269,84 @@
         spread_lo = jnp.where((lane >> 4) + 16 == j, 1.0, 0.0).astype(BF16)
         j = lax.broadcasted_iota(jnp.int32, (128, 128), 0)
         spread_scale = jnp.where((j >= 32) & (j < 35), 1.0, 0.0).astype(BF16)
-        rst[...] = dot(left, spread_scale).reshape(UNITS, 16, 128)
-        unit = lax.broadcasted_iota(jnp.int32, (UNITS * 16, 256), 0) >> 4
-        group = jnp.where(unit < V0, 1, jnp.where(unit < Q0, 2, jnp.where(unit < M0, 0, 3 + ((unit - M0) & 3))))
-        at = lax.broadcasted_iota(jnp.int32, (UNITS * 16, 256), 1) & 15
+        rst[...] = dot(left, spread_scale).reshape(23, 16, 128)
+        unit = lax.broadcasted_iota(jnp.int32, (368, 256), 0) >> 4
+        group = jnp.where(unit < 4, 1, jnp.where(unit < 8, 2, jnp.where(unit < 11, 0, 3 + ((unit - 11) & 3))))
+        at = lax.broadcasted_iota(jnp.int32, (368, 256), 1) & 15
         left_hi = jnp.where((at & 7) == group, dot(left, spread_hi), 0.0).astype(BF16)
         left_lo = jnp.where(at == group, dot(left, spread_lo), 0.0).astype(BF16)
         held = cr[...].reshape(256, 384)
-        corr[...] = (dot(left_hi, held) + dot(left_lo, held)).reshape(UNITS, 16, 384)
+        corr[...] = (dot(left_hi, held) + dot(left_lo, held)).reshape(23, 16, 384)
 
     def offset(t):
         return 16 - (16 >> t)
 
-    def rs_copy(u, c, t):
-        at = pl.ds(offset(t), 8 >> t)
-        return remote(snd.at[u, at], rcv.at[u, at], rs_s.at[u, t], rs_r.at[u, t], partners[(c + t) % 4])
+    def held_by(u):
+        return (acc2.at[u], snd2.at[u], rcv2.at[u]) if u < Q0 else (acc.at[u - Q0], snd.at[u - Q0], rcv.at[u - Q0])
+
+    def rs_copies(u, t):
+        own, out, come = held_by(u)
+        c = CLASS[u]
+        if t < 2 or u >= M0:
+            parts = [(pl.ds(offset(t), 8 >> t), t, ((c + t) % 4,))]
+        else:
+            d, e = (c + 2) % 4, (c + 3) % 4
+            parts = [(12, 2, (e,)), (13, 3, (d,)), (14, 4, (d, e))]
+        return [
+            remote(out.at[at], come.at[at], rs_s.at[u, i], rs_r.at[u, i], towards(*dims)) for at, i, dims in parts
+        ]
 
     def place_of(c, b, h):
         own = ((b >> 2) & 1, (b >> 1) & 1, b & 1, h)
         return sum(own[(c + t) % 4] << (3 - t) for t in range(4))
 
     def product(u):
-        rows, w, c = UNIT[u]
-        left = a[rows].reshape(128, 384)
-        for h in range(2):
-            value = dot(left, weights(w, h))
-            for b in range(8):
-                j = place_of(c, b, h)
-                part = value[b * 16:(b + 1) * 16]
-                if j >= 8:
-                    snd[u, j - 8] = part.astype(BF16)
-                else:
-                    acc[u, j] = part
-        start(rs_copy(u, c, 0))
+        own, out, come = held_by(u)
+        c = CLASS[u]
+        if u < Q0:
+            halves_of = [(a[u], 1, 0), (a[u], 2, 16)]
+        elif u < M0:
+            halves_of = [(a[u], 0, 0)]
+        else:
+            halves_of = [(a[4 + (u - M0) // 4], 3 + (u - M0) % 4, 0)]
+        for left, w, first in halves_of:
+            left = left.reshape(128, 384)
+            for h in range(2):
+                value = dot(left, weights(w, h))
+                for b in range(8):
+                    j = place_of(c, b, h)
+                    part = value[b * 16:(b + 1) * 16]
+                    if j >= 8:
+                        out[j - 8, pl.ds(first, 16)] = part.astype(BF16)
+                    else:
+                        own[j, pl.ds(first, 16)] = part
+        for copy in rs_copies(u, 0):
+            start(copy)
 
     def rs_step(u, t):
-        c = UNIT[u][2]
-        rs_copy(u, c, t - 1).wait_recv()
-        half, at, to = 4 >> (t - 1), offset(t - 1), offset(t)
-        snd[u, pl.ds(to, half)] = (
-            acc[u, pl.ds(half, half)] + rcv[u, pl.ds(at + half, half)].astype(F32)
+        own, out, come = held_by(u)
+        for copy in rs_copies(u, t - 1):
+            copy.wait_recv()
+        n, at, to = 8 >> (t - 1), offset(t - 1), offset(t)
+        keep = 1 if t == 2 and u < M0 else n // 2
+        out[pl.ds(to, n - keep)] = (
+            own[pl.ds(keep, n - keep)] + come[pl.ds(at + keep, n - keep)].astype(F32)
         ).astype(BF16)
-        start(rs_copy(u, c, t))
-        acc[u, pl.ds(0, half)] = acc[u, pl.ds(0, half)] + rcv[u, pl.ds(at, half)].astype(F32)
+        for copy in rs_copies(u, t):
+            start(copy)
+        own[pl.ds(0, keep)] = own[pl.ds(0, keep)] + come[pl.ds(at, keep)].astype(F32)
 
     def rs_last(u):
-        rs_copy(u, UNIT[u][2], 3).wait_recv()
-        value = acc[u, 0] + rcv[u, 14].astype(F32) + corr[u]
-        return value * jnp.concatenate([rst[u]] * 3, axis=1)
+        own, out, come = held_by(u)
+        for copy in rs_copies(u, 2 if u < M0 else 3):
+            copy.wait_recv()
+        value = own[0]
+        for i in range(12 if u < M0 else 14, 15):
+            value = value + come[i].astype(F32)
+        return value
+
+    def corrected(value, block):
+        return (value + corr[block]) * jnp.concatenate([rst[block]] * 3, axis=1)
 
     head_gain = qkg_ref[:, half_at(0, vy)]
 
@@ -326,43 +360,60 @@
             parts.append((v - mean) * lax.rsqrt(square - mean * mean + 1e-06) * head_gain[which:which + 1, cut])
         return jnp.concatenate(parts, axis=1).astype(BF16)
 
-    def kv_copy(c, s):
-        n = 1 << s
-        return remote(
-            kv.at[c, pl.ds(0, n)], kv.at[c, pl.ds(n, n)], kv_s.at[c, s], kv_r.at[c, s], partners[KV_LINKS[c][s]]
-        )
-
-    def ag_copy(k, i, s):
-        n, c = 1 << s, (i if i < 4 else A_CLASS[k])
-        return remote(
-            agb.at[k, i, pl.ds(0, n)], agb.at[k, i, pl.ds(n, n)], ag_s.at[k, i, s], ag_r.at[k, i, s],
-            partners[(c + 3 - s) % 4],
-        )
+    def kv_copies(c, s):
+        links = KV_LINKS[c]
+        if s == 0:
+            parts = [(0, 1, 0, links[:1]), (0, 2, 1, links[1:2]), (0, 3, 2, links[:2])]
+        else:
+            parts = [(pl.ds(0, 4), pl.ds(4, 4), 3, links[2:])]
+        return [
+            remote(kv.at[c, at], kv.at[c, to], kv_s.at[c, i], kv_r.at[c, i], towards(*dims)) for at, to, i, dims in parts
+        ]
+
+    def ag_copies(k, i, s):
+        c = i if i < 4 else A_CLASS[k]
+        if i < 4:
+            n = 1 << s
+            parts = [(pl.ds(0, n), pl.ds(n, n), s, ((c + 3 - s) % 4,))]
+        else:
+            n, d, e = 1 << 2 * s, (c + 3 - 2 * s) % 4, (c + 2 - 2 * s) % 4
+            parts = [
+                (pl.ds(0, n), pl.ds(n * m, n), 3 * s + m - 1, dims) for m, dims in ((1, (d,)), (2, (e,)), (3, (d, e)))
+            ]
+        return [
+            remote(agb.at[k, i, at], agb.at[k, i, to], ag_s.at[k, i, j], ag_r.at[k, i, j], towards(*dims))
+            for at, to, j, dims in parts
+        ]
 
     def ag_step(k, i, s):
         if s > 0:
-            ag_copy(k, i, s - 1).wait_recv()
-        if s < 4:
-            start(ag_copy(k, i, s))
+            for copy in ag_copies(k, i, s - 1):
+                copy.wait_recv()
+        if s < (4 if i < 4 else 2):
+            for copy in ag_copies(k, i, s):
+                start(copy)
 
     def rs_end(u):
         value = rs_last(u)
-        if u < V0:
-            kv[u, 0, pl.ds(0, 16)] = head_norm(value, 1)
-        elif u < Q0:
-            kv[u - V0, 0, pl.ds(16, 16)] = value.astype(BF16)
+        if u < Q0:
+            kv[u, 0, pl.ds(0, 16)] = head_norm(corrected(value[0:16], u), 1)
+            kv[u, 0, pl.ds(16, 16)] = corrected(value[16:32], 4 + u).astype(BF16)
+            kv_step(u, 0)
         elif u < M0:
-            qn[u - Q0] = head_norm(value, 0)
+            qn[u - Q0] = head_norm(corrected(value, 4 + u), 0)
         else:
             k, c = (u - M0) // 4, (u - M0) % 4
+            value = corrected(value, 4 + u)
             agb[k, c, 0] = (0.5 * value * (1.0 + lax.erf(value * (0.5 ** 0.5)))).astype(BF16)
             ag_step(k, c, 0)
 
     def kv_step(c, s):
         if s > 0:
-            kv_copy(c, s - 1).wait_recv()
-        if s < 3:
-            start(kv_copy(c, s))
+            for copy in kv_copies(c, s - 1):
+                copy.wait_recv()
+        if s < 2:
+            for copy in kv_copies(c, s):
+                start(copy)
 
     def attention():
         row = lax.broadcasted_iota(jnp.int32, (48, HD), 0)
@@ -388,7 +439,7 @@
     begun, loaded_wd = set(), set()
 
     def branch(k, i):
-        ag_step(k, i, 4)
+        ag_step(k, i, 4 if i < 4 else 2)
         c = i if i < 4 else A_CLASS[k]
         value = None
         for h in range(2):
@@ -433,7 +484,6 @@
         out_ref[k] = value.astype(BF16)
 
     def adapter_ready():
-        load_wa.wait()
         for way in range(2):
             for s in range(1, 5 - way):
                 across_copy(way, s).wait_recv()
@@ -477,11 +527,14 @@
             pltpu.VMEM((16, 384), BF16),
             pltpu.VMEM((16, 16, 384), BF16),
             pltpu.VMEM((4, 8, 16, 128), BF16),
-            pltpu.VMEM((UNITS, 16, 384), F32),
-            pltpu.VMEM((UNITS, 16, 128), F32),
-            pltpu.VMEM((UNITS, 8, 16, 384), F32),
-            pltpu.VMEM((UNITS, 15, 16, 384), BF16),
-            pltpu.VMEM((UNITS, 15, 16, 384), BF16),
+            pltpu.VMEM((23, 16, 384), F32),
+            pltpu.VMEM((23, 16, 128), F32),
+            pltpu.VMEM((UNITS - Q0, 8, 16, 384), F32),
+            pltpu.VMEM((UNITS - Q0, 15, 16, 384), BF16),
+            pltpu.VMEM((UNITS - Q0, 15, 16, 384), BF16),
+            pltpu.VMEM((Q0, 8, 32, 384), F32),
+            pltpu.VMEM((Q0, 15, 32, 384), BF16),
+            pltpu.VMEM((Q0, 15, 32, 384), BF16),
             pltpu.VMEM((4, 8, 32, 384), BF16),
             pltpu.VMEM((3, 16, 384), BF16),
             pltpu.VMEM((3, 5, 16, 16, 384), BF16),
@@ -495,9 +548,9 @@
             dma, dma((7, 2)), dma((5, 2)), dma,
             dma((4,)), dma((4,)),
             dma((4,)), dma((4,)),
-            dma((UNITS, 4)), dma((UNITS, 4)),
-            dma((4, 3)), dma((4, 3)),
-            dma((3, 5, 4)), dma((3, 5, 4)),
+            dma((UNITS, 5)), dma((UNITS, 5)),
+            dma((4, 4)), dma((4, 4)),
+            dma((3, 5, 6)), dma((3, 5, 6)),
             dma((3, 7)), dma((3,)),
             dma((3, 15)), dma((3,)),
             dma((7,)), dma((7,)),

time: 90.4 us -> 85.4 us (0.945); the launches traced: 89.1 us -> 85.2 us
  Pallas kernels: 86.4 us -> 82.6 us
    pallas_call x1, Pallas kernels: 86.4 us -> 82.6 us  [per_device(): pl.pallas_call(kernel, out_shape=jax.ShapeDtypeStruct((3, 32, 128), BF16)...]
where the time goes in v3:
time: 85.4 us; the launch traced here: 85.2 us
  Pallas kernels  82.6 us (97%)
  local copies, waits for them, and re-layouts  2.61 us (3%)
    pallas_call x1, Pallas kernels, per_device(): pl.pallas_call(kernel, out_shape=jax.ShapeDtypeStruct((3, 32, 128), BF16)...  82.6 us

profile of v3, /device:TPU:2, one launch (start us, length us, event | category | flops | bytes accessed | tf_op | source)
XLA Modules:
  0.0 85.2 jit_solution(9943151379855845547)
XLA Ops:
  0.0 1.2 %reshape.6.gain_ref = f32[1,384]{1,0:T(1,128)} reshape(f32[384]{0:T(512)} %param.10) | data formatting | bytes 3072 | tf_op jit(solution)/shard_map/reshape | solution.py:562
  1.2 82.6 %shard_map.91 = bf16[3,32,128]{2,1,0:T(8,128)(2,1)} custom-call(bf16[512,384]{1,0:T(8,128)(2,1)} %x_hbm.1, f32[1,384]{1,0:T(1,128)} %reshape.6.gain_ref, bf16[3,384,768]{2,1,0:T(8,128)(2,1)} %wqkv_hbm.1, f32[2,768]{1,0:T(2,128)} %qkg_ref.1, bf16[768,384]{1,0:T(8,128)(2,1)} %wout_hbm.1, bf16[384,3072]{1,0:T(8,128)(2,1)} %wup_hbm.1, ...), custom_call_target="tpu_custom_call" | custom-call | tf_op jit(solution)/shard_map/pallas_call | solution.py:515
  83.8 1.4 %copy.12 = bf16[1,3,32,128]{3,1,2,0:T(4,128)(2,1)} copy(bf16[1,3,32,128]{3,2,1,0:T(8,128)(2,1)} %bitcast.4) | data formatting | bytes 49152

commit v4 on v3

--- a/solution.py
+++ b/solution.py
@@ -12,7 +12,7 @@
 BF16 = jnp.bfloat16
 
 Q0, M0, UNITS = 4, 7, 19
-Q_CLASS, A_CLASS = (3, 0, 2), (3, 1, 2)
+Q_CLASS, A_CLASS = (0, 2, 3), (0, 2, 3)
 CLASS = (0, 1, 2, 3) + Q_CLASS + (0, 1, 2, 3) * 3
 BLOCKS = (
     [(c, 1) for c in range(4)]
@@ -20,31 +20,31 @@
     + [(4 + k, 0) for k in range(3)]
     + [(4 + k, 3 + c) for k in range(3) for c in range(4)]
 )
-KV_LINKS = ((0, 1, 2), (1, 2, 0), (2, 0, 1), (2, 1, 0))
+KV_LINKS = ((0, 1, 2), (1, 2, 0), (2, 0, 1), (2, 0, 1))
 FIRST = (3, 0, 1, 2)
 
 ORDER = (
-    ("ch",), ("x",), ("greet",), ("p", 18), ("p", 17), ("p", 16), ("p", 0), ("s", 0), ("p", 10), ("p", 12), ("p", 13),
-    ("c", 0), ("p", 2), ("p", 1), ("p", 7), ("p", 14), ("w", 0), ("r", 17, 1), ("r", 16, 1), ("s", 1), ("r", 18, 1),
-    ("p", 3), ("c", 1), ("r", 10, 1), ("r", 12, 1), ("r", 13, 1), ("r", 0, 1), ("p", 11), ("r", 14, 1), ("r", 7, 1),
-    ("p", 9), ("s", 2), ("r", 17, 2), ("r", 18, 2), ("r", 2, 1), ("r", 1, 1), ("c", 2), ("w", 1), ("r", 16, 2),
-    ("r", 10, 2), ("p", 15), ("r", 12, 2), ("p", 8), ("r", 0, 2), ("r", 3, 1), ("r", 7, 2), ("r", 11, 1), ("s", 3),
-    ("r", 9, 1), ("r", 18, 3), ("r", 13, 2), ("r", 14, 2), ("r", 17, 3), ("c", 3), ("r", 10, 3), ("p", 4), ("p", 5),
-    ("r", 1, 2), ("r", 16, 3), ("r", 15, 1), ("r", 2, 2), ("p", 6), ("r", 8, 1), ("r", 7, 3), ("r", 12, 3), ("w", 2),
-    ("s", 4), ("r", 11, 2), ("r", 3, 2), ("r", 9, 2), ("r", 14, 3), ("r", 13, 3), ("r", 15, 2), ("c", 4), ("n",),
-    ("e", 18), ("e", 17), ("r", 4, 1), ("e", 0), ("e", 1), ("e", 16), ("e", 13), ("e", 7), ("e", 2), ("r", 8, 2),
-    ("r", 11, 3), ("r", 9, 3), ("e", 12), ("g", 2, 2, 1), ("e", 10), ("r", 5, 1), ("e", 3), ("e", 14), ("r", 15, 3),
-    ("g", 0, 0, 1), ("g", 2, 3, 1), ("v", 0, 1), ("g", 2, 1, 1), ("g", 1, 2, 1), ("r", 6, 1), ("r", 4, 2),
-    ("r", 8, 3), ("e", 11), ("v", 1, 1), ("g", 1, 1, 1), ("e", 9), ("w", 3), ("g", 2, 2, 2), ("v", 2, 1), ("r", 5, 2),
-    ("e", 15), ("g", 0, 3, 1), ("g", 2, 1, 2), ("v", 3, 1), ("g", 1, 2, 2), ("g", 1, 3, 1), ("e", 8), ("g", 2, 3, 2),
-    ("g", 0, 0, 2), ("r", 6, 2), ("g", 1, 0, 1), ("g", 0, 2, 1), ("g", 1, 1, 2), ("v", 1, 2), ("g", 2, 2, 3),
-    ("v", 0, 2), ("e", 4), ("v", 2, 2), ("g", 2, 0, 1), ("e", 5), ("g", 0, 3, 2), ("g", 1, 3, 2), ("g", 1, 2, 3),
-    ("v", 3, 2), ("g", 2, 1, 3), ("g", 0, 1, 1), ("w", 4), ("g", 1, 0, 2), ("g", 0, 0, 3), ("g", 2, 3, 3),
-    ("g", 1, 1, 3), ("e", 6), ("att",), ("g", 0, 2, 2), ("g", 2, 0, 2), ("g", 0, 1, 2), ("g", 1, 3, 3), ("b", 2, 1),
-    ("g", 0, 3, 3), ("b", 2, 2), ("g", 1, 0, 3), ("b", 2, 3), ("b", 0, 0), ("b", 1, 2), ("g", 1, 4, 1), ("b", 1, 1),
-    ("g", 0, 2, 3), ("g", 0, 4, 1), ("g", 0, 1, 3), ("g", 2, 4, 1), ("g", 2, 0, 3), ("b", 1, 3), ("b", 1, 0),
-    ("b", 1, 4), ("z", 1), ("b", 0, 3), ("b", 0, 2), ("b", 0, 1), ("b", 0, 4), ("z", 0), ("b", 2, 0), ("b", 2, 4),
-    ("z", 2), ("a", 1), ("a", 0), ("d",), ("a", 2), ("f", 1), ("f", 0), ("f", 2),
+    ("ch",), ("greet",), ("p", 9), ("p", 12), ("p", 14), ("p", 11), ("p", 10), ("p", 7), ("p", 17), ("p", 0),
+    ("s", 0), ("p", 13), ("p", 16), ("p", 2), ("p", 1), ("p", 3), ("r", 12, 1), ("r", 11, 1), ("r", 14, 1), ("w", 0),
+    ("r", 9, 1), ("p", 5), ("c", 0), ("r", 7, 1), ("p", 8), ("p", 18), ("p", 15), ("r", 13, 1), ("r", 16, 1),
+    ("p", 6), ("r", 11, 2), ("r", 0, 1), ("r", 17, 1), ("r", 3, 1), ("r", 10, 1), ("s", 1), ("r", 12, 2), ("r", 9, 2),
+    ("r", 14, 2), ("c", 1), ("r", 15, 1), ("r", 2, 1), ("r", 1, 1), ("r", 13, 2), ("r", 18, 1), ("r", 6, 1),
+    ("r", 11, 3), ("r", 9, 3), ("r", 17, 2), ("r", 10, 2), ("r", 5, 1), ("r", 7, 2), ("r", 13, 3), ("p", 4),
+    ("r", 14, 3), ("r", 12, 3), ("r", 3, 2), ("r", 0, 2), ("s", 2), ("r", 16, 2), ("r", 8, 1), ("r", 18, 2), ("c", 2),
+    ("n",), ("w", 1), ("r", 2, 2), ("r", 10, 3), ("r", 17, 3), ("r", 15, 2), ("e", 13), ("e", 14), ("e", 11),
+    ("r", 5, 2), ("r", 6, 2), ("r", 1, 2), ("e", 3), ("r", 4, 1), ("r", 18, 3), ("e", 9), ("e", 12), ("r", 16, 3),
+    ("r", 7, 3), ("e", 17), ("e", 0), ("g", 1, 0, 1), ("r", 8, 2), ("e", 10), ("e", 2), ("r", 15, 3), ("e", 5),
+    ("g", 1, 3, 1), ("e", 1), ("g", 1, 2, 1), ("w", 2), ("g", 0, 2, 1), ("e", 7), ("v", 3, 1), ("x",), ("g", 1, 1, 1),
+    ("e", 16), ("e", 18), ("r", 4, 2), ("r", 8, 3), ("e", 15), ("g", 2, 2, 1), ("v", 0, 1), ("g", 1, 3, 2),
+    ("g", 1, 0, 2), ("g", 1, 2, 2), ("g", 0, 3, 1), ("v", 2, 1), ("g", 0, 0, 1), ("v", 1, 1), ("g", 2, 1, 1),
+    ("g", 1, 1, 2), ("g", 0, 2, 2), ("e", 8), ("e", 6), ("g", 2, 2, 2), ("w", 3), ("g", 2, 0, 1), ("g", 1, 3, 3),
+    ("v", 3, 2), ("g", 2, 3, 1), ("g", 1, 2, 3), ("v", 0, 2), ("e", 4), ("g", 0, 0, 2), ("g", 0, 3, 2),
+    ("g", 2, 1, 2), ("g", 1, 0, 3), ("g", 1, 1, 3), ("g", 0, 1, 1), ("v", 1, 2), ("v", 2, 2), ("att",),
+    ("g", 2, 3, 2), ("g", 2, 0, 2), ("g", 0, 3, 3), ("g", 0, 0, 3), ("g", 0, 1, 2), ("g", 1, 4, 1), ("g", 0, 4, 1),
+    ("g", 2, 3, 3), ("g", 2, 4, 1), ("g", 0, 2, 3), ("b", 1, 2), ("g", 2, 0, 3), ("b", 1, 3), ("g", 0, 1, 3),
+    ("g", 2, 2, 3), ("b", 1, 0), ("b", 0, 3), ("b", 1, 1), ("b", 0, 0), ("g", 2, 1, 3), ("b", 1, 4), ("z", 1),
+    ("b", 0, 4), ("b", 0, 2), ("b", 0, 1), ("z", 0), ("b", 2, 3), ("w", 4), ("b", 2, 4), ("b", 2, 1), ("b", 2, 2),
+    ("b", 2, 0), ("z", 2), ("a", 1), ("a", 0), ("d",), ("a", 2), ("f", 1), ("f", 0), ("f", 2),
 )
 
 
@@ -59,7 +59,7 @@
 def kernel(
     x_hbm, gain_ref, wqkv_hbm, qkg_ref, wout_hbm, wup_hbm, wdown_hbm, wad_hbm, cnt_ref,
     out_ref,
-    x, a, wv, wd, wa, stat, cpk, cr, tt, corr, rst, acc, snd, rcv, acc2, snd2, rcv2, kv, qn, agb, zs, bsum, zr, xz, tr, fs, fr,
+    x, a, wv, wd, wa, stat, cpk, cr, tt, corr, rst, acc, snd, rcv, acc2, snd2, rcv2, kv, qn, agb, zs, bsum, zr, xz, tr, fs, fr, res,
     sem_x, sem_wv, sem_wd, sem_wa,
     stat_s, stat_r, c_s, c_r, rs_s, rs_r, kv_s, kv_r, ag_s, ag_r, z_s, z_r, f_s, f_r, wz_s, wz_r, wc_s, wc_r,
 ):
@@ -112,7 +112,8 @@
         sent.append(copy)
 
     barrier = pltpu.get_barrier_semaphore()
-    for device in partners + ((dp, mx, column[0]), (dp, mx, column[6]), other):
+    greeted = partners + (towards(*FIRST[:2]), towards(*FIRST[2:]), (dp, mx, column[0]), (dp, mx, column[6]), other)
+    for device in greeted:
         pl.semaphore_signal(barrier, inc=1, device_id=device, device_id_type=MESH)
 
     load_x = pltpu.make_async_copy(x_hbm, x, sem_x)
@@ -165,7 +166,7 @@
     load_x.wait()
     xb = x[...]
     xf = xb.astype(F32)
-    gain = gain_ref[...]
+    gain = gain_ref[...].reshape(1, 384)
     centred = ((xf - jnp.mean(xf, -1, keepdims=True)) * gain).astype(BF16)
     for b in range(8):
         place = relative(b)
@@ -194,9 +195,16 @@
             loaded.add((w, h))
         return wv[w, h]
 
-    def stat_copy(s):
-        n = 1 << s
-        return remote(stat.at[pl.ds(0, n)], stat.at[pl.ds(n, n)], stat_s.at[s], stat_r.at[s], partners[FIRST[s]])
+    def spread(s):
+        n, d, e = 1 << 2 * s, FIRST[2 * s], FIRST[2 * s + 1]
+        return [
+            (pl.ds(0, n), pl.ds(n * m, n), 3 * s + m - 1, dims) for m, dims in ((1, (d,)), (2, (e,)), (3, (d, e)))
+        ]
+
+    def stat_copies(s):
+        return [
+            remote(stat.at[at], stat.at[to], stat_s.at[i], stat_r.at[i], towards(*dims)) for at, to, i, dims in spread(s)
+        ]
 
     def stat_step(s):
         if s == 0:
@@ -207,21 +215,23 @@
             lo = (x2 - hi.astype(F32)).astype(BF16)
             stat[0] = (dot_t(e0, xb) + dot_t(e1, hi) + dot_t(e1, lo))[0:2]
         else:
-            stat_copy(s - 1).wait_recv()
-        if s < 4:
-            start(stat_copy(s))
+            for copy in stat_copies(s - 1):
+                copy.wait_recv()
+        if s < 2:
+            for copy in stat_copies(s):
+                start(copy)
 
     def split(value):
         hi = value.astype(BF16).astype(F32)
         return hi, (value - hi).astype(BF16).astype(F32)
 
-    def c_copy(s):
-        if s == 0:
-            src, dst = cpk, cr.at[1]
-        else:
-            n = 1 << s
-            src, dst = cr.at[pl.ds(0, n)], cr.at[pl.ds(n, n)]
-        return remote(src, dst, c_s.at[s], c_r.at[s], partners[FIRST[s]])
+    def c_copies(s):
+        return [
+            remote(
+                cpk.at[pl.ds(0, 1)] if s == 0 and 3 in dims else cr.at[at], cr.at[to], c_s.at[i], c_r.at[i], towards(*dims)
+            )
+            for at, to, i, dims in spread(s)
+        ]
 
     def c_step(s):
         if s == 0:
@@ -237,13 +247,15 @@
                     value = part if value is None else value + part
                 sums = jnp.concatenate(split(value[0:8] + value[8:16] + value[16:24]), axis=0).astype(BF16)
                 if h == 1:
-                    cpk[...] = sums
+                    cpk[0] = sums
                 else:
                     cr[0] = sums
         else:
-            c_copy(s - 1).wait_recv()
-        if s < 4:
-            start(c_copy(s))
+            for copy in c_copies(s - 1):
+                copy.wait_recv()
+        if s < 2:
+            for copy in c_copies(s):
+                start(copy)
 
     def correct():
         sums = jnp.concatenate([stat[j][0:1] for j in range(16)], axis=0)
@@ -436,7 +448,7 @@
         for k in range(3):
             ag_step(k, 4, 0)
 
-    begun, loaded_wd = set(), set()
+    begun, loaded_wd, finished = set(), set(), set()
 
     def branch(k, i):
         ag_step(k, i, 4 if i < 4 else 2)
@@ -481,7 +493,11 @@
         value = tr[k, pl.ds(pl.multiple_of(mx * 32, 32), 32)]
         for o in range(15):
             value = value + fr[k, o].astype(F32)
-        out_ref[k] = value.astype(BF16)
+        for b in range(32):
+            res[k:k + 1, b * 128:(b + 1) * 128] = value[b:b + 1]
+        finished.add(k)
+        if len(finished) == 3:
+            out_ref[...] = res[...].astype(BF16)
 
     def adapter_ready():
         for way in range(2):
@@ -497,7 +513,7 @@
             sent.pop(0).wait_send()
 
     def greet():
-        pl.semaphore_wait(barrier, 7)
+        pl.semaphore_wait(barrier, len(greeted))
 
     events = {
         "greet": greet, "p": product, "r": rs_step, "e": rs_end, "v": kv_step, "att": attention, "g": ag_step,
@@ -512,9 +528,9 @@
 def per_device(patches, ln_gain, w_qkv, qk_gain, w_out, w_up, w_down, w_adapt, patch_counts):
     vmem, hbm = pl.BlockSpec(memory_space=pltpu.VMEM), pl.BlockSpec(memory_space=pl.ANY)
     dma = pltpu.SemaphoreType.DMA
-    out = pl.pallas_call(
+    return pl.pallas_call(
         kernel,
-        out_shape=jax.ShapeDtypeStruct((3, 32, 128), BF16),
+        out_shape=jax.ShapeDtypeStruct((3, 4096), BF16),
         in_specs=[hbm, vmem, hbm, vmem, hbm, hbm, hbm, hbm, pl.BlockSpec(memory_space=pltpu.SMEM)],
         out_specs=vmem,
         scratch_shapes=[
@@ -524,7 +540,7 @@
             pltpu.VMEM((5, 2, 384, 384), BF16),
             pltpu.VMEM((8, 384, 512), BF16),
             pltpu.VMEM((16, 2, 512), F32),
-            pltpu.VMEM((16, 384), BF16),
+            pltpu.VMEM((1, 16, 384), BF16),
             pltpu.VMEM((16, 16, 384), BF16),
             pltpu.VMEM((4, 8, 16, 128), BF16),
             pltpu.VMEM((23, 16, 384), F32),
@@ -545,9 +561,10 @@
             pltpu.VMEM((3, 512, 128), F32),
             pltpu.VMEM((3, 16, 32, 128), BF16),
             pltpu.VMEM((3, 15, 32, 128), BF16),
+            pltpu.VMEM((3, 4096), F32),
             dma, dma((7, 2)), dma((5, 2)), dma,
-            dma((4,)), dma((4,)),
-            dma((4,)), dma((4,)),
+            dma((6,)), dma((6,)),
+            dma((6,)), dma((6,)),
             dma((UNITS, 5)), dma((UNITS, 5)),
             dma((4, 4)), dma((4, 4)),
             dma((3, 5, 6)), dma((3, 5, 6)),
@@ -559,8 +576,7 @@
         compiler_params=pltpu.CompilerParams(
             collective_id=0, has_side_effects=True, vmem_limit_bytes=60 * 2**20
         ),
-    )(patches, ln_gain.reshape(1, 384), w_qkv, qk_gain, w_out, w_up, w_down, w_adapt, patch_counts)
-    return out.reshape(3, 4096)
+    )(patches, ln_gain, w_qkv, qk_gain, w_out, w_up, w_down, w_adapt, patch_counts)
 
 
 def solution(mesh):

time: 85.4 us -> 83.3 us (0.975)
  Pallas kernels: 82.6 us -> 81.1 us
  local copies, waits for them, and re-layouts: 2.61 us -> 1.39 us
    pallas_call x1, Pallas kernels: 82.6 us -> 81.1 us  [per_device(): pl.pallas_call(kernel, out_shape=jax.ShapeDtypeStruct((3, 4096), BF16), i...]
    reshape x1 -> x0, local copies, waits for them, and re-layouts: 1.24 us -> none  [per_device(): ln_gain.reshape(1, 384)]
where the time goes in v4:
time: 83.3 us; the launch traced here: 82.5 us
  Pallas kernels  81.1 us (97%)
  local copies, waits for them, and re-layouts  1.39 us (2%)
    pallas_call x1, Pallas kernels, per_device(): pl.pallas_call(kernel, out_shape=jax.ShapeDtypeStruct((3, 4096), BF16), i...  81.1 us

profile of v4, /device:TPU:2, one launch (start us, length us, event | category | flops | bytes accessed | tf_op | source)
XLA Modules:
  0.0 82.5 jit_solution(13713049133491947791)
XLA Ops:
  0.0 81.1 %shard_map.91 = bf16[3,4096]{1,0:T(4,128)(2,1)} custom-call(bf16[512,384]{1,0:T(8,128)(2,1)} %x_hbm.1, f32[384]{0:T(512)} %gain_ref.1, bf16[3,384,768]{2,1,0:T(8,128)(2,1)} %wqkv_hbm.1, f32[2,768]{1,0:T(2,128)} %qkg_ref.1, bf16[768,384]{1,0:T(8,128)(2,1)} %wout_hbm.1, bf16[384,3072]{1,0:T(8,128)(2,1)} %wup_hbm.1, bf16[3072,384]{1,0:T(8,128)(2,1)} %wdown_hbm.1, ...), custom_call_target="tpu_custom_call" | custom-call | tf_op jit(solution)/shard_map/pallas_call | solution.py:531
  81.1 1.4 %copy.11 = bf16[3,4096]{1,0:T(4,128)(2,1)} copy(bf16[3,4096]{1,0:T(4,128)(2,1)} %shard_map.91) | data formatting | bytes 49152
